TPU v7x, 32 devices: a whole 2x2x4 slice. The times are simulated.
32 devices in a mesh: tm: 8 (over z, x), rows: 4 (over y, core).
Axes of the slice: x: 2, y: 2, z: 4, core: 2. Of those that a mesh axis runs over, the one named last changes fastest.
Arguments:
- diag_blocks: float32 [16, 512, 512], P('tm', 'rows'), may hold values from -1 to 3.5, as said below
- coupling: float32 [16, 512, 512], P('tm', 'rows'), may hold values from -1.75 to 0.5
- rhs: float32 [16, 512], P('tm', 'rows'), may hold values from -0.25 to 0.25
Outputs:
- solution: float32 [16, 512], P('tm', 'rows')
- logdet_mean: float32 [], replicated
Inputs may be any that keep to these rules, and one draw needn't show every extreme that they name: Every diag_blocks[t] is symmetric, and A is positive definite.
All inputs are finite; a program needn't handle non-finite values.
Results may differ from a plain program's by a relative error of at most 0.0003.
Values sent between devices are 32-bit elements; how exact they have to be, the bound alone decides.
A program may use at most 128 MiB of HBM per device.

v0:
```python
import jax
import jax.numpy as jnp
from jax import lax
from jax.sharding import PartitionSpec as P


def shifted(block, axis, distance):
    devices = range(lax.axis_size(axis))
    route = [(i - distance, i) for i in devices if i - distance in devices]
    return lax.ppermute(block, axis, route)


def product(left_part, right_part):
    return jnp.dot(left_part, right_part, precision=lax.Precision.HIGHEST)


def cho_apply(factor, matrix):
    half_solved = lax.linalg.triangular_solve(factor, matrix, left_side=True, lower=True)
    return lax.linalg.triangular_solve(
        factor, half_solved, left_side=True, lower=True, transpose_a=True
    )


def apply_vector(factor, vector):
    return cho_apply(factor, vector[:, None])[:, 0]


def eliminate(pivot_block, left_link, right_link, vector, row_start, row_count):
    factor = jnp.linalg.cholesky(pivot_block)
    log_det = 2.0 * jnp.sum(jnp.log(jnp.diagonal(factor)))
    left_rows = lax.dynamic_slice_in_dim(left_link, row_start, row_count, 0)
    right_cols = lax.dynamic_slice_in_dim(right_link, row_start, row_count, 1)
    solved = cho_apply(factor, jnp.concatenate([left_rows.T, right_cols], axis=1))
    solved_vector = apply_vector(factor, vector)
    from_left = solved[:, :row_count]
    from_right = solved[:, row_count:]
    highest = lax.Precision.HIGHEST
    left_diag = jnp.einsum("ki,jk->ij", from_left, left_link, precision=highest)
    new_left = -jnp.einsum("ki,kj->ij", from_left, right_link, precision=highest)
    right_diag = jnp.einsum("ki,kj->ij", from_right, right_link, precision=highest)
    left_rhs = product(left_rows, solved_vector)
    right_rhs = jnp.einsum("ki,k->i", right_cols, solved_vector, precision=highest)
    return (factor, log_det, left_diag, new_left, left_rhs, right_diag, right_rhs)


def local(diag_blocks, coupling, rhs):
    group_steps, shard_rows, state_width = diag_blocks.shape
    group_count = lax.axis_size("tm")
    group_index = lax.axis_index("tm")
    row_start = lax.axis_index("rows") * shard_rows
    level_count = group_count.bit_length() - 1
    not_last = jnp.where(group_index == group_count - 1, 0.0, 1.0).astype(jnp.float32)

    def along_time(values, offset):
        return shifted(values, "tm", offset)

    def solved_from(values, offset):
        return shifted(values, "tm", offset)

    sep_diag = diag_blocks[0]
    sep_rhs = rhs[0]
    pivot_block = diag_blocks[1]
    left_link = coupling[0]
    vector = rhs[1]
    step_index = 1
    right_link = coupling[step_index]
    right_link = right_link * not_last
    full_pivot, full_left, full_right, full_vector = lax.all_gather(
        (pivot_block, left_link, right_link, vector), "rows", axis=0, tiled=True
    )
    factor, log_det, left_diag, new_left, left_rhs, right_diag, right_rhs = eliminate(
        full_pivot, full_left, full_right, full_vector, row_start, shard_rows
    )
    chain = [(factor, full_left, full_right, full_vector)]
    log_total = log_det
    sep_diag = sep_diag - left_diag
    sep_rhs = sep_rhs - left_rhs
    left_link = new_left
    incoming_diag, incoming_rhs = along_time((right_diag, right_rhs), 1)
    sep_diag = sep_diag - incoming_diag
    sep_rhs = sep_rhs - incoming_rhs
    upper_link = left_link
    sep_diag, upper_link, sep_rhs = (
        lax.all_gather(sep_diag, "rows", axis=0, tiled=True),
        lax.all_gather(upper_link, "rows", axis=0, tiled=True),
        lax.all_gather(sep_rhs, "rows", axis=0, tiled=True),
    )
    col_start, col_count = (0, state_width)
    levels_kept = []
    for level_index in range(level_count):
        stride = 1 << level_index
        is_pivot = group_index % (2 * stride) == stride
        survives = group_index % (2 * stride) == 0
        from_below = along_time(upper_link, stride)
        full_pivot, full_left, full_right, full_vector = (sep_diag, from_below, upper_link, sep_rhs)
        factor, log_det, left_diag, new_left, left_rhs, right_diag, right_rhs = eliminate(
            full_pivot, full_left, full_right, full_vector, col_start, col_count
        )
        levels_kept.append((is_pivot, factor, full_left, full_right, full_vector))
        log_total = log_total + jnp.where(is_pivot, log_det, 0.0)
        up_diag, up_link, up_rhs = along_time((left_diag, new_left, left_rhs), -stride)
        down_diag, down_rhs = along_time((right_diag, right_rhs), stride)
        sep_diag = jnp.where(survives, sep_diag - up_diag - down_diag, sep_diag)
        upper_link = jnp.where(survives, up_link, upper_link)
        sep_rhs = jnp.where(survives, sep_rhs - up_rhs - down_rhs, sep_rhs)
    top_pivot, top_vector = (sep_diag, sep_rhs)
    top_factor = jnp.linalg.cholesky(top_pivot)
    top_det = 2.0 * jnp.sum(jnp.log(jnp.diagonal(top_factor)))
    log_total = log_total + jnp.where(group_index == 0, top_det, 0.0)
    states = apply_vector(top_factor, top_vector)
    for level_index in reversed(range(level_count)):
        stride = 1 << level_index
        is_pivot, factor, full_left, full_right, full_vector = levels_kept[level_index]
        state_below = solved_from(states, stride)
        state_above = solved_from(states, -stride)
        new_state = apply_vector(
            factor, full_vector - product(state_below, full_left) - product(full_right, state_above)
        )
        states = jnp.where(is_pivot, new_state, states)
    following = solved_from(states, -1)
    rows_out = [lax.dynamic_slice_in_dim(states, row_start, shard_rows, 0)] * group_steps
    step_index = 1
    factor, full_left, full_right, full_vector = chain[step_index - 1]
    following = apply_vector(
        factor, full_vector - product(states, full_left) - product(full_right, following)
    )
    rows_out[step_index] = lax.dynamic_slice_in_dim(following, row_start, shard_rows, 0)
    solution = jnp.stack(rows_out, axis=0)
    total_det = lax.psum(log_total, "tm")
    return (solution, total_det / (group_steps * group_count * state_width))


def solution(mesh):
    in_specs = (P("tm", "rows", None), P("tm", "rows", None), P("tm", "rows"))
    out_specs = (P("tm", "rows"), P())
    return jax.shard_map(local, mesh=mesh, in_specs=in_specs, out_specs=out_specs, check_vma=False)
```

profile of v0, /device:TPU:0, one launch (start us, length us, event | category | flops | bytes accessed | tf_op | source)
XLA Modules:
  0.0 1235.8 jit_solution(8387934566385280009)
XLA Ops:
  30.8 16.6 %all-gather.15.cloned.1.call-done = f32[1,512,512]{1,2,0:T(8,128)} async-done(((f32[1,128,512]{1,2,0:T(8,128)}), f32[1,512,512]{1,2,0:T(8,128)}) %all-gather.15.cloned.1.call-update) | async-done | bytes 1048592 | tf_op jit(solution)/shard_map/all_gather | solution.py:68
  49.4 11.7 cholesky.550
  71.7 11.7 cholesky.569
  94.2 11.7 cholesky.590
  117.0 21.2 %cholesky.607 = f32[128,128]{1,0:T(8,128)S(1)} custom-call(f32[128,128]{1,0:T(8,128)S(1)} %convolution_subtract_fusion.27), custom_call_target="Cholesky" | custom-call | tf_op jit(solution)/shard_map/jit(cholesky)/cholesky | solution.py:29
  150.1 39.3 %custom-call.37 = f32[4,128,128]{1,2,0:T(8,128)S(1)} custom-call(f32[4,128,128]{2,1,0:T(8,128)S(1)} %get-tuple-element.46), custom_call_target="InvertDiagBlocksLowerTriangular" | custom-call | tf_op jit(solution)/shard_map/triangular_solve | solution.py:19
  241.3 11.7 cholesky.622
  342.9 40.8 %custom-call.116 = f32[4,128,128]{1,2,0:T(8,128)} custom-call(f32[4,128,128]{2,1,0:T(8,128)} %get-tuple-element.188), custom_call_target="InvertDiagBlocksLowerTriangular" | custom-call | tf_op jit(solution)/shard_map/triangular_solve/custom-call.10 | solution.py:19
  436.9 44.3 %collective-permute-done.6 = f32[512]{0:T(512)S(1)} collective-permute-done((f32[512]{0:T(512)S(1)}, f32[512]{0:T(512)S(1)}, u32[]{:S(2)}, u32[]{:S(2)}) %collective-permute-start.6) | collective-permute-done | bytes 2080 | tf_op jit(solution)/shard_map/ppermute | solution.py:10
  557.7 11.9 cholesky.751
  582.1 39.3 %custom-call.114 = f32[4,128,128]{1,2,0:T(8,128)S(1)} custom-call(f32[4,128,128]{2,1,0:T(8,128)S(1)} %get-tuple-element.186), custom_call_target="InvertDiagBlocksLowerTriangular" | custom-call | tf_op jit(solution)/shard_map/triangular_solve/custom-call.10 | solution.py:19
  632.1 20.1 %collective-permute-done.8 = f32[512,512]{1,0:T(8,128)S(1)} collective-permute-done((f32[512,512]{1,0:T(8,128)}, f32[512,512]{1,0:T(8,128)S(1)}, u32[]{:S(2)}, u32[]{:S(2)}) %collective-permute-start.8) | collective-permute-done | bytes 1048608 | tf_op jit(solution)/shard_map/ppermute | solution.py:10
  703.8 11.7 cholesky.766
  754.8 13.2 %cholesky.806 = f32[128,128]{1,0:T(8,128)} custom-call(f32[128,128]{1,0:T(8,128)} %cholesky.954), custom_call_target="Cholesky" | custom-call | tf_op jit(solution)/shard_map/jit(cholesky)/cholesky | solution.py:29
  783.6 12.1 cholesky.823
  812.7 40.8 %custom-call.112 = f32[4,128,128]{1,2,0:T(8,128)} custom-call(f32[4,128,128]{2,1,0:T(8,128)} %get-tuple-element.184), custom_call_target="InvertDiagBlocksLowerTriangular" | custom-call | tf_op jit(solution)/shard_map/triangular_solve/custom-call.10 | solution.py:19
  872.9 15.3 %collective-permute-done.14 = f32[512,512]{1,0:T(8,128)S(1)} collective-permute-done((f32[512,512]{1,0:T(8,128)}, f32[512,512]{1,0:T(8,128)S(1)}, u32[]{:S(2)}, u32[]{:S(2)}) %collective-permute-start.14) | collective-permute-done | bytes 1048608 | tf_op jit(solution)/shard_map/ppermute | solution.py:10
  945.1 11.7 cholesky.838
  1000.9 13.2 %cholesky.878 = f32[128,128]{1,0:T(8,128)} custom-call(f32[128,128]{1,0:T(8,128)} %cholesky.967), custom_call_target="Cholesky" | custom-call | tf_op jit(solution)/shard_map/jit(cholesky)/cholesky | solution.py:107
  1030.6 11.8 cholesky.895
  1050.0 14.0 %while.50 = (s32[]{:T(128)}, f32[512,512]{1,0:T(8,128)}, s32[4,2]{0,1:T(2,128)S(1)}, f32[4,128,128]{2,1,0:T(8,128)}, s32[]{:T(128)}) while((s32[]{:T(128)}, f32[512,512]{1,0:T(8,128)}, s32[4,2]{0,1:T(2,128)S(1)}, f32[4,128,128]{2,1,0:T(8,128)}, s32[]{:T(128)}) %tuple.219), condition=%wide.while_cond.1.clone.3, body=%wide.while_body.1.clone.3.sunk | while | flops 2 | bytes 132205 | solution.py:19
  1064.0 40.7 %custom-call.110 = f32[4,128,128]{1,2,0:T(8,128)} custom-call(f32[4,128,128]{2,1,0:T(8,128)} %get-tuple-element.182), custom_call_target="InvertDiagBlocksLowerTriangular" | custom-call | tf_op jit(solution)/shard_map/triangular_solve/custom-call.10 | solution.py:19
  1149.9 27.2 %collective-permute-start.21 = (f32[512]{0:T(512)S(1)}, f32[512]{0:T(512)S(1)}, u32[]{:S(2)}, u32[]{:S(2)}) collective-permute-start(f32[512]{0:T(512)S(1)} %broadcast_select_fusion.2), channel_id=1, source_target_pairs={{0,8},{4,12},{8,16},{12,20},{16,24},{20,28},{1,9},{5,13},{9,17},{1... | collective-permute-start | bytes 6152 | tf_op jit(solution)/shard_map/ppermute | solution.py:10
  1185.9 24.0 %psum.7 = f32[]{:T(128)} all-reduce(f32[]{:T(128)S(6)} %add.90), channel_id=1, replica_groups=mesh['tm'=8,'rows'=4] {'tm'}, use_global_device_ids=true, to_apply=%region_13.19 | all-reduce | flops 1 | bytes 8 | tf_op jit(solution)/shard_map/psum | solution.py:129
  (637 shorter events, 736.0 us)
Async XLA Ops:
  7.2 21.9 %all-gather.17.cloned.1.call-start = ((), (), s32[]{:S(2)}) async-start(), calls=%async_computation.3 | async-start | bytes 1310720 | tf_op jit(solution)/shard_map/all_gather | solution.py:68
  9.1 38.3 %all-gather.15.cloned.1.call-start = ((), (), s32[]{:S(2)}) async-start(), calls=%async_computation.2 | async-start | bytes 1310720 | tf_op jit(solution)/shard_map/all_gather | solution.py:68
  11.1 178.6 %all-gather.19.cloned.1.call-start = ((), (), s32[]{:S(2)}) async-start(), calls=%async_computation.4 | async-start | bytes 1310720 | tf_op jit(solution)/shard_map/all_gather | solution.py:68
  11.8 219.2 %all-gather.13.cloned.1.call-start = ((), (), s32[]{:S(2)}) async-start(), calls=%async_computation.1 | async-start | bytes 1310720 | tf_op jit(solution)/shard_map/all_gather | solution.py:85
  199.7 38.7 %all-gather.11.cloned.1.call-start = ((), (), s32[]{:S(2)}) async-start(), calls=%async_computation | async-start | bytes 1310720 | tf_op jit(solution)/shard_map/all_gather | solution.py:84
  233.6 158.7 %collective-permute-start.2 = (f32[512,512]{1,0:T(8,128)}, f32[512,512]{1,0:T(8,128)S(1)}, u32[]{:S(2)}, u32[]{:S(2)}) collective-permute-start(f32[512,512]{1,0:T(8,128)} %copy.56), channel_id=1, source_target_pairs={{0,4},{4,8},{8,12},{12,16},{16,20},{20,24},{24,28},{1,5},{5,9},{9,... | collective-permute-start | bytes 3145736 | tf_op jit(solution)/shard_map/ppermute | solution.py:10
  409.9 71.4 %collective-permute-start.3 = (f32[512,512]{0,1:T(8,128)}, f32[512,512]{0,1:T(8,128)}, u32[]{:S(2)}, u32[]{:S(2)}) collective-permute-start(f32[512,512]{0,1:T(8,128)} %fusion.147), channel_id=1, source_target_pairs={{4,0},{8,4},{12,8},{16,12},{20,16},{24,20},{28,24},{5,1},{9,5},{13... | collective-permute-start | bytes 3145736 | tf_op jit(solution)/shard_map/ppermute | solution.py:10
  414.2 67.0 %collective-permute-start.4 = (f32[512,512]{0,1:T(8,128)}, f32[512,512]{0,1:T(8,128)}, u32[]{:S(2)}, u32[]{:S(2)}) collective-permute-start(f32[512,512]{0,1:T(8,128)} %fusion.97), channel_id=1, source_target_pairs={{0,4},{4,8},{8,12},{12,16},{16,20},{20,24},{24,28},{1,5},{5,9},{9,... | collective-permute-start | bytes 3145736 | tf_op jit(solution)/shard_map/ppermute | solution.py:10
  427.7 53.5 %collective-permute-start.6 = (f32[512]{0:T(512)S(1)}, f32[512]{0:T(512)S(1)}, u32[]{:S(2)}, u32[]{:S(2)}) collective-permute-start(f32[512]{0:T(512)S(1)} %bitcast.1314), channel_id=1, source_target_pairs={{0,4},{4,8},{8,12},{12,16},{16,20},{20,24},{24,28},{1,5},{5,9},{9,... | collective-permute-start | bytes 6152 | tf_op jit(solution)/shard_map/ppermute | solution.py:10
  431.2 50.0 %collective-permute-start.5 = (f32[512]{0:T(512)S(1)}, f32[512]{0:T(512)S(1)}, u32[]{:S(2)}, u32[]{:S(2)}) collective-permute-start(f32[512]{0:T(512)S(1)} %bitcast.1316), channel_id=1, source_target_pairs={{4,0},{8,4},{12,8},{16,12},{20,16},{24,20},{28,24},{5,1},{9,5},{13... | collective-permute-start | bytes 6152 | tf_op jit(solution)/shard_map/ppermute | solution.py:10
  435.5 187.6 %collective-permute-start.7 = (f32[512,512]{0,1:T(8,128)}, f32[512,512]{0,1:T(8,128)}, u32[]{:S(2)}, u32[]{:S(2)}) collective-permute-start(f32[512,512]{0,1:T(8,128)} %convolution_negate_fusion.1), channel_id=1, source_target_pairs={{4,0},{8,4},{12,8},{16,12},{20,16},{24,20},{28,24},{5,1},{9,5},{13... | collective-permute-start | bytes 3145736 | tf_op jit(solution)/shard_map/ppermute | solution.py:10
  626.0 26.3 %collective-permute-start.8 = (f32[512,512]{1,0:T(8,128)}, f32[512,512]{1,0:T(8,128)S(1)}, u32[]{:S(2)}, u32[]{:S(2)}) collective-permute-start(f32[512,512]{1,0:T(8,128)} %copy.64), channel_id=1, source_target_pairs={{0,8},{4,12},{8,16},{12,20},{16,24},{20,28},{1,9},{5,13},{9,17},{1... | collective-permute-start | bytes 3145736 | tf_op jit(solution)/shard_map/ppermute | solution.py:10
  670.6 29.0 %collective-permute-start.9 = (f32[512,512]{0,1:T(8,128)S(1)}, f32[512,512]{0,1:T(8,128)S(1)}, u32[]{:S(2)}, u32[]{:S(2)}) collective-permute-start(f32[512,512]{0,1:T(8,128)S(1)} %fusion.144), channel_id=1, source_target_pairs={{8,0},{12,4},{16,8},{20,12},{24,16},{28,20},{9,1},{13,5},{17,9},{2... | collective-permute-start | bytes 3145736 | tf_op jit(solution)/shard_map/ppermute | solution.py:10
  671.9 27.7 %collective-permute-start.10 = (f32[512,512]{0,1:T(8,128)S(1)}, f32[512,512]{0,1:T(8,128)S(1)}, u32[]{:S(2)}, u32[]{:S(2)}) collective-permute-start(f32[512,512]{0,1:T(8,128)S(1)} %fusion.95), channel_id=1, source_target_pairs={{0,8},{4,12},{8,16},{12,20},{16,24},{20,28},{1,9},{5,13},{9,17},{1... | collective-permute-start | bytes 3145736 | tf_op jit(solution)/shard_map/ppermute | solution.py:10
  678.1 20.5 %collective-permute-start.12 = (f32[512]{0:T(512)S(1)}, f32[512]{0:T(512)S(1)}, u32[]{:S(2)}, u32[]{:S(2)}) collective-permute-start(f32[512]{0:T(512)S(1)} %bitcast.1315), channel_id=1, source_target_pairs={{0,8},{4,12},{8,16},{12,20},{16,24},{20,28},{1,9},{5,13},{9,17},{1... | collective-permute-start | bytes 6152 | tf_op jit(solution)/shard_map/ppermute | solution.py:10
  687.2 172.2 %collective-permute-start.13 = (f32[512,512]{0,1:T(8,128)}, f32[512,512]{0,1:T(8,128)}, u32[]{:S(2)}, u32[]{:S(2)}) collective-permute-start(f32[512,512]{0,1:T(8,128)} %convolution_negate_fusion), channel_id=1, source_target_pairs={{8,0},{12,4},{16,8},{20,12},{24,16},{28,20},{9,1},{13,5},{17,9},{2... | collective-permute-start | bytes 3145736 | tf_op jit(solution)/shard_map/ppermute | solution.py:10
  862.2 26.1 %collective-permute-start.14 = (f32[512,512]{1,0:T(8,128)}, f32[512,512]{1,0:T(8,128)S(1)}, u32[]{:S(2)}, u32[]{:S(2)}) collective-permute-start(f32[512,512]{1,0:T(8,128)} %copy.72), channel_id=1, source_target_pairs={{0,16},{4,20},{8,24},{12,28},{1,17},{5,21},{9,25},{13,29},{2,18},{... | collective-permute-start | bytes 3145736 | tf_op jit(solution)/shard_map/ppermute | solution.py:10
  908.6 28.0 %collective-permute-start.15 = (f32[512,512]{0,1:T(8,128)}, f32[512,512]{0,1:T(8,128)}, u32[]{:S(2)}, u32[]{:S(2)}) collective-permute-start(f32[512,512]{0,1:T(8,128)} %fusion.93), channel_id=1, source_target_pairs={{16,0},{20,4},{24,8},{28,12},{17,1},{21,5},{25,9},{29,13},{18,2},{... | collective-permute-start | bytes 3145736 | tf_op jit(solution)/shard_map/ppermute | solution.py:10
  909.9 26.7 %collective-permute-start.16 = (f32[512,512]{0,1:T(8,128)}, f32[512,512]{0,1:T(8,128)}, u32[]{:S(2)}, u32[]{:S(2)}) collective-permute-start(f32[512,512]{0,1:T(8,128)} %fusion.91), channel_id=1, source_target_pairs={{0,16},{4,20},{8,24},{12,28},{1,17},{5,21},{9,25},{13,29},{2,18},{... | collective-permute-start | bytes 3145736 | tf_op jit(solution)/shard_map/ppermute | solution.py:10
  918.6 17.5 %collective-permute-start.18 = (f32[512]{0:T(512)S(1)}, f32[512]{0:T(512)S(1)}, u32[]{:S(2)}, u32[]{:S(2)}) collective-permute-start(f32[512]{0:T(512)S(1)} %bitcast.1310), channel_id=1, source_target_pairs={{0,16},{4,20},{8,24},{12,28},{1,17},{5,21},{9,25},{13,29},{2,18},{... | collective-permute-start | bytes 6152 | tf_op jit(solution)/shard_map/ppermute | solution.py:10
  1119.7 16.9 %collective-permute-start.20 = (f32[512]{0:T(512)S(1)}, f32[512]{0:T(512)S(1)}, u32[]{:S(2)}, u32[]{:S(2)}) collective-permute-start(f32[512]{0:T(512)S(1)} %bitcast.1303), channel_id=1, source_target_pairs={{16,0},{20,4},{24,8},{28,12},{17,1},{21,5},{25,9},{29,13},{18,2},{... | collective-permute-start | bytes 6152 | tf_op jit(solution)/shard_map/ppermute | solution.py:10
  1142.8 34.3 %collective-permute-start.22 = (f32[512]{0:T(512)S(1)}, f32[512]{0:T(512)S(1)}, u32[]{:S(2)}, u32[]{:S(2)}) collective-permute-start(f32[512]{0:T(512)S(1)} %broadcast_select_fusion.2), channel_id=1, source_target_pairs={{8,0},{12,4},{16,8},{20,12},{24,16},{28,20},{9,1},{13,5},{17,9},{2... | collective-permute-start | bytes 6152 | tf_op jit(solution)/shard_map/ppermute | solution.py:10
  1149.9 28.5 %collective-permute-start.21 = (f32[512]{0:T(512)S(1)}, f32[512]{0:T(512)S(1)}, u32[]{:S(2)}, u32[]{:S(2)}) collective-permute-start(f32[512]{0:T(512)S(1)} %broadcast_select_fusion.2), channel_id=1, source_target_pairs={{0,8},{4,12},{8,16},{12,20},{16,24},{20,28},{1,9},{5,13},{9,17},{1... | collective-permute-start | bytes 6152 | tf_op jit(solution)/shard_map/ppermute | solution.py:10
  1183.3 29.6 %collective-permute-start.24 = (f32[512]{0:T(512)S(1)}, f32[512]{0:T(512)S(1)}, u32[]{:S(2)}, u32[]{:S(2)}) collective-permute-start(f32[512]{0:T(512)S(1)} %broadcast_select_fusion.3), channel_id=1, source_target_pairs={{4,0},{8,4},{12,8},{16,12},{20,16},{24,20},{28,24},{5,1},{9,5},{13... | collective-permute-start | bytes 6152 | tf_op jit(solution)/shard_map/ppermute | solution.py:10
  (66 other events, 1418.9 us)
Sparse Core Ops, SparseCore 0:
  9.6 19.4 all-gather.16
  30.6 16.8 all-gather.14
  49.0 16.8 all-gather.18
  199.8 16.8 all-gather.12
  218.1 16.9 all-gather.10
where the time goes:
time: 1250 us; the launch traced here: 1240 us
  other arithmetic  648 us (52%)
  matrix products  174 us (14%)
  waiting for transfers between devices  129 us (10%)
  local copies, waits for them, and re-layouts  116 us (9%)
  starting transfers between devices  98.7 us (8%)
  blocking collectives  35 us (3%)
  between operations  34 us (3%)
    another operation x59, other arithmetic, eliminate(): factor = jnp.linalg.cholesky(pivot_block)  331 us
    another operation x19, other arithmetic, cho_apply(): lax.linalg.triangular_solve(factor, half_solved, left_side=True, lower=Tr...  211 us
    ppermute x26, waiting for transfers between devices, shifted(): return lax.ppermute(block, axis, route)  102 us
    ppermute x26, starting transfers between devices, shifted(): return lax.ppermute(block, axis, route)  98.5 us
    another operation x15, other arithmetic, local(): top_factor = jnp.linalg.cholesky(top_pivot)  86.7 us
    another operation x91, matrix products, cho_apply(): lax.linalg.triangular_solve(factor, matrix, left_side=True, lower=True)  56 us
    another operation x91, matrix products, cho_apply(): lax.linalg.triangular_solve(factor, half_solved, left_side=True, lower=Tr...  46 us
    another operation x49, local copies, waits for them, and re-layouts, cho_apply(): lax.linalg.triangular_solve(factor, half_solved, left_side=True, lower=Tr...  42.7 us
  transfers between devices with their start and end apart: 31, of which 13 were waited for; matrix products, arithmetic and copies ran while one was open for 54% of the time, Pallas kernels for 0%

commit v1 on v0

v1 whole, which is shorter than its diff:
```python
import functools

import jax
import jax.numpy as jnp
from jax import lax
from jax.experimental import pallas as pl
from jax.experimental.pallas import tpu as pltpu
from jax.sharding import PartitionSpec as P

HIGHEST = lax.Precision.HIGHEST
TILE = 128
PANELS = 4


def dot(left, right, contract):
    return lax.dot_general(
        left, right, ((contract[0:1], contract[1:2]), ((), ())),
        precision=HIGHEST, preferred_element_type=jnp.float32,
    )


def sweep_tile(tiles):
    count = len(tiles)
    sub = lax.broadcasted_iota(jnp.int32, (8, TILE), 0)
    lane = lax.broadcasted_iota(jnp.int32, (8, TILE), 1)

    def row_of(value, j):
        return jnp.broadcast_to(value[j:j + 1, :], (8, TILE))

    def col_of(value, k):
        return jnp.broadcast_to(value[:, k:k + 1], (8, TILE))

    def one_panel(tiles, pivots, q):
        first = 8 * q
        in_panel = (lane >= first) & (lane < first + 8)
        minus_unit = jnp.where(lane - first == sub, -1.0, 0.0).astype(jnp.float32)
        panel = tiles[q]
        columns = [col_of(panel, first + m) for m in range(8)]
        swept = jnp.where(in_panel, minus_unit, panel)
        for j in range(8):
            pivot = row_of(columns[j], j)
            inverse = 1.0 / pivot
            pivots = jnp.where(lane == first + j, pivot, pivots)
            at_j = sub == j
            scale = jnp.where(at_j, -inverse, columns[j] * inverse)
            for m in range(j + 1, 8):
                columns[m] = jnp.where(at_j, 0.0, columns[m]) - scale * row_of(columns[m], j)
            swept = jnp.where(at_j, 0.0, swept) - scale * row_of(swept, j)
        rows = [row_of(swept, m) for m in range(8)]
        out = []
        for t in [(q + 1 + i) % count for i in range(count)]:
            if t == q:
                out.append((t, swept))
                continue
            parts = [col_of(tiles[t], first + m) * rows[m] for m in range(8)]
            while len(parts) > 1:
                parts = [a + b for a, b in zip(parts[::2], parts[1::2])]
            out.append((t, jnp.where(in_panel, 0.0, tiles[t]) - parts[0]))
        return [value for _, value in sorted(out, key=lambda pair: pair[0])], pivots

    def step(_, carry):
        tiles, pivots = list(carry[:-1]), carry[-1]
        for q in range(PANELS):
            tiles, pivots = one_panel(tiles, pivots, q)
        shift = TILE - 8 * PANELS
        tiles = tiles[PANELS:] + tiles[:PANELS]
        tiles = [pltpu.roll(value, shift, 1) for value in tiles]
        return (*tiles, pltpu.roll(pivots, shift, 1))

    ones = jnp.ones((8, TILE), jnp.float32)
    carry = lax.fori_loop(0, count // PANELS, step, (*tiles, ones))
    return list(carry[:-1]), carry[-1]


def inverse_kernel(size, matrix_ref, inverse_ref, logdet_ref, tile_ref, cols_ref):
    blocks = size // TILE
    inverse_ref[...] = matrix_ref[...]
    logdet_ref[...] = jnp.zeros((8, TILE), jnp.float32)

    @pl.loop(0, blocks)
    def _(block):
        start = pl.multiple_of(block * TILE, TILE)
        here = pl.ds(start, TILE)
        tiles = [
            inverse_ref[pl.ds(pl.multiple_of(start + 8 * t, 8), 8), here]
            for t in range(TILE // 8)
        ]
        tiles, pivots = sweep_tile(tiles)
        logdet_ref[...] += jnp.log(pivots)
        for t, value in enumerate(tiles):
            tile_ref[8 * t:8 * t + 8, :] = value
        cols_ref[...] = inverse_ref[:, here]
        cols_ref[here, :] = jnp.zeros((TILE, TILE), jnp.float32)
        inverse_ref[:, here] = jnp.zeros((size, TILE), jnp.float32)
        swept = -dot(tile_ref[...], inverse_ref[here, :], (1, 0))
        inverse_ref[here, :] = swept
        inverse_ref[here, here] = tile_ref[...]
        swept = inverse_ref[here, :]
        inverse_ref[...] -= dot(cols_ref[...], swept, (1, 0))

    inverse_ref[...] = -inverse_ref[...]


def inverted(matrix):
    size = matrix.shape[0]
    inverse, logs = pl.pallas_call(
        functools.partial(inverse_kernel, size),
        out_shape=(
            jax.ShapeDtypeStruct((size, size), jnp.float32),
            jax.ShapeDtypeStruct((8, TILE), jnp.float32),
        ),
        in_specs=[pl.BlockSpec(memory_space=pltpu.VMEM)],
        out_specs=(pl.BlockSpec(memory_space=pltpu.VMEM),) * 2,
        scratch_shapes=[
            pltpu.VMEM((TILE, TILE), jnp.float32),
            pltpu.VMEM((size, TILE), jnp.float32),
        ],
        compiler_params=pltpu.CompilerParams(vmem_limit_bytes=24 << 20),
        cost_estimate=pl.CostEstimate(
            flops=80 * size**3, bytes_accessed=8 * size * size, transcendentals=size
        ),
    )(matrix)
    return inverse, jnp.sum(logs[0])


def updates_kernel(rows, inverse_ref, left_ref, right_ref, both_ref, vector_ref, up_ref, down_ref):
    solved = dot(both_ref[...], inverse_ref[...], (1, 0))
    from_right = dot(solved, right_ref[...], (1, 0))
    up_ref[0:rows, :] = dot(solved[0:rows], left_ref[...], (1, 1))
    up_ref[rows:2 * rows, :] = -from_right[0:rows]
    down_ref[0:rows, :] = from_right[rows:]
    vector = dot(vector_ref[...], solved, (1, 1))
    up_ref[2 * rows:, :] = jnp.zeros_like(up_ref[2 * rows:, :])
    up_ref[2 * rows:, 0:rows] = vector[:, 0:rows]
    down_ref[rows:, :] = jnp.zeros_like(down_ref[rows:, :])
    down_ref[rows:, 0:rows] = vector[:, rows:]


def updates(inverse, left, right, left_rows, right_rows, vector):
    rows, size = left_rows.shape
    return pl.pallas_call(
        functools.partial(updates_kernel, rows),
        out_shape=(
            jax.ShapeDtypeStruct((2 * rows + 8, size), jnp.float32),
            jax.ShapeDtypeStruct((rows + 8, size), jnp.float32),
        ),
        in_specs=[pl.BlockSpec(memory_space=pltpu.VMEM)] * 5,
        out_specs=(pl.BlockSpec(memory_space=pltpu.VMEM),) * 2,
        compiler_params=pltpu.CompilerParams(vmem_limit_bytes=24 << 20),
    )(
        inverse, left, right, jnp.concatenate([left_rows, right_rows]),
        jnp.broadcast_to(vector[None], (8, size)),
    )


def product(left_part, right_part):
    return jnp.dot(left_part, right_part, precision=HIGHEST)


def shifted(block, axis, distance):
    devices = range(lax.axis_size(axis))
    route = [(i - distance, i) for i in devices if i - distance in devices]
    return lax.ppermute(block, axis, route)


def local(diag_blocks, coupling, rhs):
    group_steps, rows, size = diag_blocks.shape
    parts = lax.axis_size("rows")
    group_count = lax.axis_size("tm")
    group_index = lax.axis_index("tm")
    row_start = lax.axis_index("rows") * rows
    level_count = group_count.bit_length() - 1
    not_last = jnp.where(group_index == group_count - 1, 0.0, 1.0).astype(jnp.float32)

    def my_rows(matrix):
        return lax.dynamic_slice_in_dim(matrix, row_start, rows, 0)

    def my_columns_t(matrix):
        return lax.dynamic_slice_in_dim(matrix, row_start, rows, 1).T

    def gathered(packed):
        whole = lax.all_gather(packed, "rows", axis=0)
        diag = whole[:, :rows].reshape(size, size)
        link = whole[:, rows:2 * rows].reshape(size, size)
        vector = whole[:, 2 * rows, :rows].reshape(size)
        return diag, link, vector

    def as_row(vector):
        return jnp.pad(vector[None], ((0, 7), (0, size - rows)))

    right_rows_first = coupling[1] * not_last
    pivot = lax.all_gather(diag_blocks[1], "rows", axis=0, tiled=True)
    links = lax.all_gather(
        jnp.concatenate([coupling[0], right_rows_first, as_row(rhs[1])]), "rows", axis=0
    )
    left = links[:, :rows].reshape(size, size)
    right = links[:, rows:2 * rows].reshape(size, size)
    vector = links[:, 2 * rows, :rows].reshape(size)
    inverse, log_total = inverted(pivot)
    up, down = updates(inverse, left, right, coupling[0], my_columns_t(right), vector)
    chain = (inverse, left, right, vector)
    down = shifted(down, "tm", 1)
    packed = jnp.concatenate([
        diag_blocks[0] - up[:rows] - down[:rows],
        up[rows:2 * rows],
        as_row(rhs[0]) - up[2 * rows:] - down[rows:],
    ])
    levels_kept = []
    for level_index in range(level_count):
        stride = 1 << level_index
        is_pivot = group_index % (2 * stride) == stride
        survives = group_index % (2 * stride) == 0
        diag, right, vector = gathered(packed)
        left = shifted(right, "tm", stride)
        inverse, log_det = inverted(diag)
        up, down = updates(inverse, left, right, my_rows(left), my_columns_t(right), vector)
        levels_kept.append((is_pivot, inverse, left, right, vector))
        log_total = log_total + jnp.where(is_pivot, log_det, 0.0)
        up = shifted(up, "tm", -stride)
        down = shifted(down, "tm", stride)
        new = jnp.concatenate([
            packed[:rows] - up[:rows] - down[:rows],
            up[rows:2 * rows],
            packed[2 * rows:] - up[2 * rows:] - down[rows:],
        ])
        packed = jnp.where(survives, new, packed)
    diag, _, vector = gathered(packed)
    inverse, log_det = inverted(diag)
    log_total = log_total + jnp.where(group_index == 0, log_det, 0.0)
    total_det = lax.psum(log_total, "tm")
    states = product(inverse, vector)
    for level_index in reversed(range(level_count)):
        stride = 1 << level_index
        is_pivot, inverse, left, right, vector = levels_kept[level_index]
        below = shifted(states, "tm", stride)
        above = shifted(states, "tm", -stride)
        new_state = product(inverse, vector - product(below, left) - product(right, above))
        states = jnp.where(is_pivot, new_state, states)
    inverse, left, right, vector = chain
    following = shifted(states, "tm", -1)
    following = product(inverse, vector - product(states, left) - product(right, following))
    solution = jnp.stack([my_rows(states), my_rows(following)], axis=0)
    return (solution, total_det / (group_steps * group_count * size))


def solution(mesh):
    in_specs = (P("tm", "rows", None), P("tm", "rows", None), P("tm", "rows"))
    out_specs = (P("tm", "rows"), P())
    return jax.shard_map(local, mesh=mesh, in_specs=in_specs, out_specs=out_specs, check_vma=False)
```

time: 1250 us -> 500 us (0.40)
  other arithmetic: 648 us -> 26.1 us
  matrix products: 174 us -> 16.7 us
  Pallas kernels: 0 us -> 134 us
  local copies, waits for them, and re-layouts: 116 us -> 52 us
  starting transfers between devices: 98.7 us -> 53.7 us
  waiting for transfers between devices: 129 us -> 166 us
  between operations: 34 us -> 20 us
    another operation x95 -> x1, other arithmetic: 630 us -> 0.58 us  [local(): solution = jnp.stack([my_rows(states), my_rows(following)], axis=0)]
    pallas_call x0 -> x9, Pallas kernels: none -> 134 us  [the longest x5 118 us: inverted(): pl.pallas_call(functools.partial(inverse_kernel, size), out_shape=(jax.Sh...]
    another operation x212 -> x0, matrix products: 132 us -> none  [the longest x91 56 us: cho_apply(): lax.linalg.triangular_solve(factor, matrix, left_side=True, lower=True)]
    all_gather x5 -> x6, waiting for transfers between devices: 26.9 us -> 123 us  [the longest x4 105 us: gathered(): whole = lax.all_gather(packed, 'rows', axis=0)]
    ppermute x26 -> x17, waiting for transfers between devices: 102 us -> 43 us  [shifted(): return lax.ppermute(block, axis, route)]
    another operation x82 -> x2, local copies, waits for them, and re-layouts: 53.3 us -> 0.16 us  [local(): solution = jnp.stack([my_rows(states), my_rows(following)], axis=0)]
    ppermute x26 -> x17, starting transfers between devices: 98.5 us -> 53.4 us  [shifted(): return lax.ppermute(block, axis, route)]
    gather x5 -> x0, local copies, waits for them, and re-layouts: 35.5 us -> none  [the longest x4 31 us: eliminate(): log_det = 2.0 * jnp.sum(jnp.log(jnp.diagonal(factor)))]
  transfers between devices with their start and end apart: 31 -> 23, of which waited for: 13 -> 14; matrix products, arithmetic and copies ran while one was open for 54% -> 4% of each run, Pallas kernels for 0% -> 19%
where the time goes in v1:
time: 500 us; the launch traced here: 492 us
  waiting for transfers between devices  166 us (33%)
  Pallas kernels  134 us (27%)
  starting transfers between devices  53.7 us (11%)
  local copies, waits for them, and re-layouts  52 us (10%)
  other arithmetic  26.1 us (5%)
  blocking collectives  24.5 us (5%)
  between operations  20 us (4%)
  matrix products  16.7 us (3%)
    pallas_call x5, Pallas kernels, inverted(): pl.pallas_call(functools.partial(inverse_kernel, size), out_shape=(jax.Sh...  118 us
    all_gather x4, waiting for transfers between devices, gathered(): whole = lax.all_gather(packed, 'rows', axis=0)  105 us
    ppermute x17, starting transfers between devices, shifted(): return lax.ppermute(block, axis, route)  53.4 us
    ppermute x17, waiting for transfers between devices, shifted(): return lax.ppermute(block, axis, route)  43 us
    psum x1, blocking collectives, local(): total_det = lax.psum(log_total, 'tm')  24.5 us
    unnamed x65, local copies, waits for them, and re-layouts  17.8 us
    all_gather x1, waiting for transfers between devices, local(): pivot = lax.all_gather(diag_blocks[1], 'rows', axis=0, tiled=True)  17.3 us
    dot_general x13, matrix products, product(): return jnp.dot(left_part, right_part, precision=HIGHEST)  16.7 us
  transfers between devices with their start and end apart: 23, of which 14 were waited for; matrix products, arithmetic and copies ran while one was open for 4% of the time, Pallas kernels for 19%

profile of v1, /device:TPU:0, one launch (start us, length us, event | category | flops | bytes accessed | tf_op | source)
XLA Modules:
  0.0 492.5 jit_solution(11167581681599947605)
XLA Ops:
  11.7 17.3 %all-gather.16.cloned.1.call-done = f32[1,512,512]{2,1,0:T(8,128)} async-done(((f32[1,128,512]{2,1,0:T(8,128)}), f32[1,512,512]{2,1,0:T(8,128)}) %all-gather.16.cloned.1.call-update) | async-done | bytes 1048592 | tf_op jit(solution)/shard_map/all_gather | solution.py:192
  30.2 23.5 %shard_map.50 = (f32[512,512]{1,0:T(8,128)S(1)}, f32[8,128]{1,0:T(8,128)S(1)}) custom-call(f32[512,512]{1,0:T(8,128)S(1)} %bitcast.126), custom_call_target="tpu_custom_call" | custom-call | flops 10737418240 | bytes 2097152 | tf_op jit(solution)/shard_map/pallas_call | solution.py:106
  66.9 6.3 %collective-permute-done = f32[136,512]{1,0:T(8,128)S(1)} collective-permute-done((f32[136,512]{1,0:T(8,128)S(1)}, f32[136,512]{1,0:T(8,128)S(1)}, u32[]{:S(2)}, u32[]{:S(2)}) %collective-permute-start) | collective-permute-done | bytes 278560 | tf_op jit(solution)/shard_map/ppermute | solution.py:163
  75.7 24.1 %all-gather.20.cloned.1.call-done = f32[1056,512]{1,0:T(8,128)} async-done(((f32[264,512]{1,0:T(8,128)}), f32[1056,512]{1,0:T(8,128)}) %all-gather.20.cloned.1.call-update) | async-done | bytes 2162704 | tf_op jit(solution)/shard_map/all_gather | solution.py:182
  109.2 23.5 %shard_map.52 = (f32[512,512]{1,0:T(8,128)S(1)}, f32[8,128]{1,0:T(8,128)S(1)}) custom-call(f32[512,512]{1,0:T(8,128)S(1)} %bitcast.123), custom_call_target="tpu_custom_call" | custom-call | flops 10737418240 | bytes 2097152 | tf_op jit(solution)/shard_map/pallas_call | solution.py:106
  138.4 4.2 shard_map.53
  144.0 4.6 collective-permute-start.3
  148.5 16.2 %collective-permute-done.3 = f32[136,512]{1,0:T(8,128)S(1)} collective-permute-done((f32[136,512]{1,0:T(8,128)S(1)}, f32[136,512]{1,0:T(8,128)S(1)}, u32[]{:S(2)}, u32[]{:S(2)}) %collective-permute-start.3) | collective-permute-done | bytes 278560 | tf_op jit(solution)/shard_map/ppermute | solution.py:163
  169.2 23.2 %all-gather.10.cloned.1.call-done = f32[4,264,512]{2,1,0:T(8,128)} async-done(((f32[1,264,512]{2,1,0:T(8,128)}), f32[4,264,512]{2,1,0:T(8,128)}) %all-gather.10.cloned.1.call-update) | async-done | bytes 2162704 | tf_op jit(solution)/shard_map/all_gather | solution.py:182
  203.6 23.5 %shard_map.54 = (f32[512,512]{1,0:T(8,128)S(1)}, f32[8,128]{1,0:T(8,128)S(1)}) custom-call(f32[512,512]{1,0:T(8,128)S(1)} %bitcast.124), custom_call_target="tpu_custom_call" | custom-call | flops 10737418240 | bytes 2097152 | tf_op jit(solution)/shard_map/pallas_call | solution.py:106
  235.7 4.2 shard_map.55
  241.4 5.3 %collective-permute-start.6 = (f32[136,512]{1,0:T(8,128)S(1)}, f32[136,512]{1,0:T(8,128)}, u32[]{:S(2)}, u32[]{:S(2)}) collective-permute-start(f32[136,512]{1,0:T(8,128)S(1)} %get-tuple-element.28), channel_id=1, source_target_pairs={{0,8},{4,12},{8,16},{12,20},{16,24},{20,28},{1,9},{5,13},{9,17},{1... | collective-permute-start | bytes 835592 | tf_op jit(solution)/shard_map/ppermute | solution.py:163
  251.7 4.6 collective-permute-done.5
  259.8 22.1 %all-gather.12.cloned.1.call-done = f32[4,264,512]{2,1,0:T(8,128)} async-done(((f32[1,264,512]{2,1,0:T(8,128)}), f32[4,264,512]{2,1,0:T(8,128)}) %all-gather.12.cloned.1.call-update) | async-done | bytes 2162704 | tf_op jit(solution)/shard_map/all_gather | solution.py:182
  285.9 4.6 collective-permute-start.7
  294.1 23.5 %shard_map.56 = (f32[512,512]{1,0:T(8,128)S(1)}, f32[8,128]{1,0:T(8,128)S(1)}) custom-call(f32[512,512]{1,0:T(8,128)S(1)} %bitcast.125), custom_call_target="tpu_custom_call" | custom-call | flops 10737418240 | bytes 2097152 | tf_op jit(solution)/shard_map/pallas_call | solution.py:106
  328.4 4.2 shard_map.57
  333.9 6.9 %collective-permute-start.9 = (f32[136,512]{1,0:T(8,128)S(1)}, f32[136,512]{1,0:T(8,128)}, u32[]{:S(2)}, u32[]{:S(2)}) collective-permute-start(f32[136,512]{1,0:T(8,128)S(1)} %get-tuple-element.31), channel_id=1, source_target_pairs={{0,16},{4,20},{8,24},{12,28},{1,17},{5,21},{9,25},{13,29},{2,18},{... | collective-permute-start | bytes 835592 | tf_op jit(solution)/shard_map/ppermute | solution.py:163
  345.9 4.0 collective-permute-done.8
  355.2 36.0 %all-gather.14.cloned.1.call-done = f32[4,264,512]{2,1,0:T(8,128)} async-done(((f32[1,264,512]{2,1,0:T(8,128)}), f32[4,264,512]{2,1,0:T(8,128)}) %all-gather.14.cloned.1.call-update) | async-done | bytes 2162704 | tf_op jit(solution)/shard_map/all_gather | solution.py:182
  392.5 23.5 %shard_map.58 = (f32[512,512]{1,0:T(8,128)S(1)}, f32[8,128]{1,0:T(8,128)S(1)}) custom-call(f32[512,512]{1,0:T(8,128)S(1)} %bitcast.122), custom_call_target="tpu_custom_call" | custom-call | flops 10737418240 | bytes 2097152 | tf_op jit(solution)/shard_map/pallas_call | solution.py:106
  420.3 5.6 %collective-permute-start.10 = (f32[512]{0:T(512)S(1)}, f32[512]{0:T(512)S(1)}, u32[]{:S(2)}, u32[]{:S(2)}) collective-permute-start(f32[512]{0:T(512)S(1)} %bitcast.147), channel_id=1, source_target_pairs={{0,16},{4,20},{8,24},{12,28},{1,17},{5,21},{9,25},{13,29},{2,18},{... | collective-permute-start | bytes 6152 | tf_op jit(solution)/shard_map/ppermute | solution.py:163
  433.0 4.8 collective-permute-start.12
  444.7 24.5 %psum.7 = f32[]{:T(128)} all-reduce(f32[]{:T(128)S(6)} %add.49), channel_id=1, replica_groups=mesh['tm'=8,'rows'=4] {'tm'}, use_global_device_ids=true, to_apply=%region_5.6 | all-reduce | flops 1 | bytes 8 | tf_op jit(solution)/shard_map/psum | solution.py:230
  (182 shorter events, 132.2 us)
Async XLA Ops:
  7.2 21.9 %all-gather.16.cloned.1.call-start = ((), (), s32[]{:S(2)}) async-start(), calls=%async_computation.3 | async-start | bytes 1310720 | tf_op jit(solution)/shard_map/all_gather | solution.py:192
  8.9 44.9 %all-gather.18.cloned.1.call-start = ((), (), s32[]{:S(2)}) async-start(), calls=%async_computation.4 | async-start | bytes 2703360 | tf_op jit(solution)/shard_map/all_gather | solution.py:193
  11.7 88.1 %all-gather.20.cloned.1.call-start = ((), (), s32[]{:S(2)}) async-start(), calls=%async_computation.5 | async-start | bytes 2703360 | tf_op jit(solution)/shard_map/all_gather | solution.py:182
  63.4 9.7 %collective-permute-start = (f32[136,512]{1,0:T(8,128)S(1)}, f32[136,512]{1,0:T(8,128)S(1)}, u32[]{:S(2)}, u32[]{:S(2)}) collective-permute-start(f32[136,512]{1,0:T(8,128)S(1)} %get-tuple-element.22), channel_id=1, source_target_pairs={{0,4},{4,8},{8,12},{12,16},{16,20},{20,24},{24,28},{1,5},{5,9},{9,... | collective-permute-start | bytes 835592 | tf_op jit(solution)/shard_map/ppermute | solution.py:163
  75.7 116.7 %all-gather.10.cloned.1.call-start = ((), (), s32[]{:S(2)}) async-start(), calls=%async_computation | async-start | bytes 2703360 | tf_op jit(solution)/shard_map/all_gather | solution.py:182
  102.9 29.9 %collective-permute-start.1 = (f32[512,512]{0,1:T(8,128)}, f32[512,512]{0,1:T(8,128)S(1)}, u32[]{:S(2)}, u32[]{:S(2)}) collective-permute-start(f32[512,512]{0,1:T(8,128)} %copy.30), channel_id=1, source_target_pairs={{0,4},{4,8},{8,12},{12,16},{16,20},{20,24},{24,28},{1,5},{5,9},{9,... | collective-permute-start | bytes 3145736 | tf_op jit(solution)/shard_map/ppermute | solution.py:163
  142.7 22.0 %collective-permute-start.2 = (f32[264,512]{1,0:T(8,128)}, f32[264,512]{1,0:T(8,128)S(1)}, u32[]{:S(2)}, u32[]{:S(2)}) collective-permute-start(f32[264,512]{1,0:T(8,128)} %get-tuple-element.24), channel_id=1, source_target_pairs={{4,0},{8,4},{12,8},{16,12},{20,16},{24,20},{28,24},{5,1},{9,5},{13... | collective-permute-start | bytes 1622024 | tf_op jit(solution)/shard_map/ppermute | solution.py:163
  144.0 20.7 %collective-permute-start.3 = (f32[136,512]{1,0:T(8,128)S(1)}, f32[136,512]{1,0:T(8,128)S(1)}, u32[]{:S(2)}, u32[]{:S(2)}) collective-permute-start(f32[136,512]{1,0:T(8,128)S(1)} %get-tuple-element.25), channel_id=1, source_target_pairs={{0,4},{4,8},{8,12},{12,16},{16,20},{20,24},{24,28},{1,5},{5,9},{9,... | collective-permute-start | bytes 835592 | tf_op jit(solution)/shard_map/ppermute | solution.py:163
  169.1 112.8 %all-gather.12.cloned.1.call-start = ((), (), s32[]{:S(2)}) async-start(), calls=%async_computation.1 | async-start | bytes 2703360 | tf_op jit(solution)/shard_map/all_gather | solution.py:182
  196.4 30.8 %collective-permute-start.4 = (f32[512,512]{0,1:T(8,128)}, f32[512,512]{0,1:T(8,128)S(1)}, u32[]{:S(2)}, u32[]{:S(2)}) collective-permute-start(f32[512,512]{0,1:T(8,128)} %copy.31), channel_id=1, source_target_pairs={{0,8},{4,12},{8,16},{12,20},{16,24},{20,28},{1,9},{5,13},{9,17},{1... | collective-permute-start | bytes 3145736 | tf_op jit(solution)/shard_map/ppermute | solution.py:163
  240.0 16.4 %collective-permute-start.5 = (f32[264,512]{1,0:T(8,128)}, f32[264,512]{1,0:T(8,128)S(1)}, u32[]{:S(2)}, u32[]{:S(2)}) collective-permute-start(f32[264,512]{1,0:T(8,128)} %get-tuple-element.27), channel_id=1, source_target_pairs={{8,0},{12,4},{16,8},{20,12},{24,16},{28,20},{9,1},{13,5},{17,9},{2... | collective-permute-start | bytes 1622024 | tf_op jit(solution)/shard_map/ppermute | solution.py:163
  241.4 10.3 %collective-permute-start.6 = (f32[136,512]{1,0:T(8,128)S(1)}, f32[136,512]{1,0:T(8,128)}, u32[]{:S(2)}, u32[]{:S(2)}) collective-permute-start(f32[136,512]{1,0:T(8,128)S(1)} %get-tuple-element.28), channel_id=1, source_target_pairs={{0,8},{4,12},{8,16},{12,20},{16,24},{20,28},{1,9},{5,13},{9,17},{1... | collective-permute-start | bytes 835592 | tf_op jit(solution)/shard_map/ppermute | solution.py:163
  259.8 131.5 %all-gather.14.cloned.1.call-start = ((), (), s32[]{:S(2)}) async-start(), calls=%async_computation.2 | async-start | bytes 2703360 | tf_op jit(solution)/shard_map/all_gather | solution.py:182
  285.9 32.7 %collective-permute-start.7 = (f32[512,512]{0,1:T(8,128)}, f32[512,512]{0,1:T(8,128)S(1)}, u32[]{:S(2)}, u32[]{:S(2)}) collective-permute-start(f32[512,512]{0,1:T(8,128)} %copy.32), channel_id=1, source_target_pairs={{0,16},{4,20},{8,24},{12,28},{1,17},{5,21},{9,25},{13,29},{2,18},{... | collective-permute-start | bytes 3145736 | tf_op jit(solution)/shard_map/ppermute | solution.py:163
  332.6 17.2 %collective-permute-start.8 = (f32[264,512]{1,0:T(8,128)}, f32[264,512]{1,0:T(8,128)}, u32[]{:S(2)}, u32[]{:S(2)}) collective-permute-start(f32[264,512]{1,0:T(8,128)} %get-tuple-element.30), channel_id=1, source_target_pairs={{16,0},{20,4},{24,8},{28,12},{17,1},{21,5},{25,9},{29,13},{18,2},{... | collective-permute-start | bytes 1622024 | tf_op jit(solution)/shard_map/ppermute | solution.py:163
  333.9 12.0 %collective-permute-start.9 = (f32[136,512]{1,0:T(8,128)S(1)}, f32[136,512]{1,0:T(8,128)}, u32[]{:S(2)}, u32[]{:S(2)}) collective-permute-start(f32[136,512]{1,0:T(8,128)S(1)} %get-tuple-element.31), channel_id=1, source_target_pairs={{0,16},{4,20},{8,24},{12,28},{1,17},{5,21},{9,25},{13,29},{2,18},{... | collective-permute-start | bytes 835592 | tf_op jit(solution)/shard_map/ppermute | solution.py:163
  417.8 8.2 %collective-permute-start.11 = (f32[512]{0:T(512)S(1)}, f32[512]{0:T(512)S(1)}, u32[]{:S(2)}, u32[]{:S(2)}) collective-permute-start(f32[512]{0:T(512)S(1)} %bitcast.146), channel_id=1, source_target_pairs={{16,0},{20,4},{24,8},{28,12},{17,1},{21,5},{25,9},{29,13},{18,2},{... | collective-permute-start | bytes 6152 | tf_op jit(solution)/shard_map/ppermute | solution.py:163
  420.3 6.9 %collective-permute-start.10 = (f32[512]{0:T(512)S(1)}, f32[512]{0:T(512)S(1)}, u32[]{:S(2)}, u32[]{:S(2)}) collective-permute-start(f32[512]{0:T(512)S(1)} %bitcast.147), channel_id=1, source_target_pairs={{0,16},{4,20},{8,24},{12,28},{1,17},{5,21},{9,25},{13,29},{2,18},{... | collective-permute-start | bytes 6152 | tf_op jit(solution)/shard_map/ppermute | solution.py:163
  430.4 7.4 %collective-permute-start.13 = (f32[512]{0:T(512)S(1)}, f32[512]{0:T(512)S(1)}, u32[]{:S(2)}, u32[]{:S(2)}) collective-permute-start(f32[512]{0:T(512)S(1)} %broadcast_select_fusion), channel_id=1, source_target_pairs={{8,0},{12,4},{16,8},{20,12},{24,16},{28,20},{9,1},{13,5},{17,9},{2... | collective-permute-start | bytes 6152 | tf_op jit(solution)/shard_map/ppermute | solution.py:163
  433.0 5.8 %collective-permute-start.12 = (f32[512]{0:T(512)S(1)}, f32[512]{0:T(512)S(1)}, u32[]{:S(2)}, u32[]{:S(2)}) collective-permute-start(f32[512]{0:T(512)S(1)} %broadcast_select_fusion), channel_id=1, source_target_pairs={{0,8},{4,12},{8,16},{12,20},{16,24},{20,28},{1,9},{5,13},{9,17},{1... | collective-permute-start | bytes 6152 | tf_op jit(solution)/shard_map/ppermute | solution.py:163
  442.0 39.6 %copy-start.1 = (f32[4,128,512]{2,1,0:T(8,128)S(1)}, f32[4,128,512]{2,1,0:T(8,128)}, u32[]{:S(2)}) copy-start(f32[4,128,512]{2,1,0:T(8,128)} %copy-done) | copy-start | bytes 3145732
  442.0 29.3 %collective-permute-start.15 = (f32[512]{0:T(512)S(1)}, f32[512]{0:T(512)S(1)}, u32[]{:S(2)}, u32[]{:S(2)}) collective-permute-start(f32[512]{0:T(512)S(1)} %broadcast_select_fusion.1), channel_id=1, source_target_pairs={{4,0},{8,4},{12,8},{16,12},{20,16},{24,20},{28,24},{5,1},{9,5},{13... | collective-permute-start | bytes 6152 | tf_op jit(solution)/shard_map/ppermute | solution.py:163
  469.9 2.7 collective-permute-start.14
  475.9 5.7 %collective-permute-start.16 = (f32[512]{0:T(512)S(1)}, f32[512]{0:T(512)S(1)}, u32[]{:S(2)}, u32[]{:S(2)}) collective-permute-start(f32[512]{0:T(512)S(1)} %broadcast_select_fusion.2), channel_id=1, source_target_pairs={{4,0},{8,4},{12,8},{16,12},{20,16},{24,20},{28,24},{5,1},{9,5},{13... | collective-permute-start | bytes 6152 | tf_op jit(solution)/shard_map/ppermute | solution.py:163
  (31 other events, 188.6 us)
Sparse Core Ops, SparseCore 0:
  9.6 19.4 all-gather.15
  30.6 22.9 all-gather.17
  75.8 23.9 all-gather.19
  169.2 23.0 all-gather.9
  259.9 21.9 all-gather.11
  352.8 38.3 all-gather.13

commit v2 on v1

--- a/solution.py
+++ b/solution.py
@@ -120,36 +120,39 @@
             flops=80 * size**3, bytes_accessed=8 * size * size, transcendentals=size
         ),
     )(matrix)
-    return inverse, jnp.sum(logs[0])
-
-
-def updates_kernel(rows, inverse_ref, left_ref, right_ref, both_ref, vector_ref, up_ref, down_ref):
+    return inverse, logs
+
+
+def updates_kernel(
+    rows, inverse_ref, left_ref, right_ref, both_ref, vector_ref, logs_ref, tail_ref,
+    up_ref, down_ref, link_ref,
+):
     solved = dot(both_ref[...], inverse_ref[...], (1, 0))
     from_right = dot(solved, right_ref[...], (1, 0))
     up_ref[0:rows, :] = dot(solved[0:rows], left_ref[...], (1, 1))
-    up_ref[rows:2 * rows, :] = -from_right[0:rows]
+    link_ref[...] = -from_right[0:rows]
     down_ref[0:rows, :] = from_right[rows:]
     vector = dot(vector_ref[...], solved, (1, 1))
-    up_ref[2 * rows:, :] = jnp.zeros_like(up_ref[2 * rows:, :])
-    up_ref[2 * rows:, 0:rows] = vector[:, 0:rows]
-    down_ref[rows:, :] = jnp.zeros_like(down_ref[rows:, :])
+    size = up_ref.shape[1]
+    up_ref[rows:, :] = jnp.zeros((8, size), jnp.float32)
+    up_ref[rows:, 0:rows] = vector[:, 0:rows]
+    up_ref[rows:, size - TILE:] = logs_ref[...] - tail_ref[:, size - TILE:]
+    down_ref[rows:, :] = jnp.zeros((8, size), jnp.float32)
     down_ref[rows:, 0:rows] = vector[:, rows:]
 
 
-def updates(inverse, left, right, left_rows, right_rows, vector):
+def updates(inverse, left, right, left_rows, right_rows, vector, logs, tail):
     rows, size = left_rows.shape
+    message = jax.ShapeDtypeStruct((rows + 8, size), jnp.float32)
     return pl.pallas_call(
         functools.partial(updates_kernel, rows),
-        out_shape=(
-            jax.ShapeDtypeStruct((2 * rows + 8, size), jnp.float32),
-            jax.ShapeDtypeStruct((rows + 8, size), jnp.float32),
-        ),
-        in_specs=[pl.BlockSpec(memory_space=pltpu.VMEM)] * 5,
-        out_specs=(pl.BlockSpec(memory_space=pltpu.VMEM),) * 2,
+        out_shape=(message, message, jax.ShapeDtypeStruct((rows, size), jnp.float32)),
+        in_specs=[pl.BlockSpec(memory_space=pltpu.VMEM)] * 7,
+        out_specs=(pl.BlockSpec(memory_space=pltpu.VMEM),) * 3,
         compiler_params=pltpu.CompilerParams(vmem_limit_bytes=24 << 20),
     )(
         inverse, left, right, jnp.concatenate([left_rows, right_rows]),
-        jnp.broadcast_to(vector[None], (8, size)),
+        jnp.broadcast_to(vector[None], (8, size)), logs, tail,
     )
 
 
@@ -165,7 +168,6 @@
 
 def local(diag_blocks, coupling, rhs):
     group_steps, rows, size = diag_blocks.shape
-    parts = lax.axis_size("rows")
     group_count = lax.axis_size("tm")
     group_index = lax.axis_index("tm")
     row_start = lax.axis_index("rows") * rows
@@ -178,69 +180,60 @@
     def my_columns_t(matrix):
         return lax.dynamic_slice_in_dim(matrix, row_start, rows, 1).T
 
-    def gathered(packed):
-        whole = lax.all_gather(packed, "rows", axis=0)
-        diag = whole[:, :rows].reshape(size, size)
-        link = whole[:, rows:2 * rows].reshape(size, size)
-        vector = whole[:, 2 * rows, :rows].reshape(size)
-        return diag, link, vector
+    def gathered(part):
+        return lax.all_gather(part, "rows", axis=0, tiled=True)
 
     def as_row(vector):
         return jnp.pad(vector[None], ((0, 7), (0, size - rows)))
 
-    right_rows_first = coupling[1] * not_last
-    pivot = lax.all_gather(diag_blocks[1], "rows", axis=0, tiled=True)
-    links = lax.all_gather(
-        jnp.concatenate([coupling[0], right_rows_first, as_row(rhs[1])]), "rows", axis=0
+    def eliminated(diag_part, left_part, right_part, vector_part, tail):
+        diag = gathered(diag_part)
+        left, right, vector = gathered(left_part), gathered(right_part), gathered(vector_part)
+        inverse, logs = inverted(diag)
+        up, down, link = updates(
+            inverse, left, right, left_part, my_columns_t(right), vector, logs, tail
+        )
+        return up, down, link, (inverse, left, right, vector)
+
+    tail = jnp.zeros((8, size), jnp.float32)
+    up, down, link, chain = eliminated(
+        diag_blocks[1], coupling[0], coupling[1] * not_last, rhs[1], tail
     )
-    left = links[:, :rows].reshape(size, size)
-    right = links[:, rows:2 * rows].reshape(size, size)
-    vector = links[:, 2 * rows, :rows].reshape(size)
-    inverse, log_total = inverted(pivot)
-    up, down = updates(inverse, left, right, coupling[0], my_columns_t(right), vector)
-    chain = (inverse, left, right, vector)
     down = shifted(down, "tm", 1)
-    packed = jnp.concatenate([
-        diag_blocks[0] - up[:rows] - down[:rows],
-        up[rows:2 * rows],
-        as_row(rhs[0]) - up[2 * rows:] - down[rows:],
-    ])
+    left, right = shifted(link, "tm", 1), link
+    diag = diag_blocks[0] - up[:rows] - down[:rows]
+    tail = as_row(rhs[0]) - up[rows:] - down[rows:]
     levels_kept = []
     for level_index in range(level_count):
         stride = 1 << level_index
         is_pivot = group_index % (2 * stride) == stride
-        survives = group_index % (2 * stride) == 0
-        diag, right, vector = gathered(packed)
-        left = shifted(right, "tm", stride)
-        inverse, log_det = inverted(diag)
-        up, down = updates(inverse, left, right, my_rows(left), my_columns_t(right), vector)
-        levels_kept.append((is_pivot, inverse, left, right, vector))
-        log_total = log_total + jnp.where(is_pivot, log_det, 0.0)
-        up = shifted(up, "tm", -stride)
-        down = shifted(down, "tm", stride)
-        new = jnp.concatenate([
-            packed[:rows] - up[:rows] - down[:rows],
-            up[rows:2 * rows],
-            packed[2 * rows:] - up[2 * rows:] - down[rows:],
-        ])
-        packed = jnp.where(survives, new, packed)
-    diag, _, vector = gathered(packed)
-    inverse, log_det = inverted(diag)
-    log_total = log_total + jnp.where(group_index == 0, log_det, 0.0)
-    total_det = lax.psum(log_total, "tm")
-    states = product(inverse, vector)
+        up, down, link, kept = eliminated(diag, left, right, tail[0, :rows], tail)
+        levels_kept.append((is_pivot, kept))
+        up, down = shifted(up, "tm", -stride), shifted(down, "tm", stride)
+        diag = diag - up[:rows] - down[:rows]
+        tail = tail - up[rows:] - down[rows:]
+        if level_index < level_count - 1:
+            left, right = shifted(link, "tm", stride), shifted(link, "tm", -stride)
+    vector = gathered(tail[0, :rows])
+    inverse, logs = inverted(gathered(diag))
+    total = jnp.sum(logs[0] - tail[0, size - TILE:])
+    states = jnp.concatenate([product(inverse, vector), jnp.full((TILE,), total)])
     for level_index in reversed(range(level_count)):
         stride = 1 << level_index
-        is_pivot, inverse, left, right, vector = levels_kept[level_index]
+        is_pivot, (inverse, left, right, vector) = levels_kept[level_index]
         below = shifted(states, "tm", stride)
         above = shifted(states, "tm", -stride)
-        new_state = product(inverse, vector - product(below, left) - product(right, above))
-        states = jnp.where(is_pivot, new_state, states)
+        new_state = product(
+            inverse, vector - product(below[:size], left) - product(right, above[:size])
+        )
+        states = jnp.where(is_pivot, jnp.concatenate([new_state, below[size:]]), states)
+    total = states[size]
+    states = states[:size]
     inverse, left, right, vector = chain
     following = shifted(states, "tm", -1)
     following = product(inverse, vector - product(states, left) - product(right, following))
     solution = jnp.stack([my_rows(states), my_rows(following)], axis=0)
-    return (solution, total_det / (group_steps * group_count * size))
+    return (solution, total / (group_steps * group_count * size))
 
 
 def solution(mesh):

time: 500 us -> 431 us (0.86); the launches traced: 492 us -> 429 us
  waiting for transfers between devices: 166 us -> 133 us
  other arithmetic: 26.1 us -> 12.9 us
  local copies, waits for them, and re-layouts: 52 us -> 42.6 us
  matrix products: 16.7 us -> 10.2 us
    all_gather x6 -> x13, waiting for transfers between devices: 123 us -> 52 us  [gathered(): return lax.all_gather(part, 'rows', axis=0, tiled=True)]
    ppermute x17 -> x19, waiting for transfers between devices: 43 us -> 80.6 us  [shifted(): return lax.ppermute(block, axis, route)]
    all_gather x0 -> x5, blocking collectives: none -> 26.3 us  [gathered(): return lax.all_gather(part, 'rows', axis=0, tiled=True)]
    psum x1 -> x0, blocking collectives: 24.5 us -> none  [local(): total_det = lax.psum(log_total, 'tm')]
    slice x11 -> x16, local copies, waits for them, and re-layouts: 15.6 us -> 1.27 us  [the longest x1 0.72 us: local(): diag_blocks[1]]
    unnamed x65 -> x104, local copies, waits for them, and re-layouts: 17.8 us -> 27.5 us
    all_gather x0 -> x3, local copies, waits for them, and re-layouts: none -> 7.68 us  [gathered(): return lax.all_gather(part, 'rows', axis=0, tiled=True)]
    ppermute x3 -> x0, local copies, waits for them, and re-layouts: 6.69 us -> none  [shifted(): return lax.ppermute(block, axis, route)]
  transfers between devices with their start and end apart: 23 -> 32, of which waited for: 14 -> 20; matrix products, arithmetic and copies ran while one was open for 4% -> 6% of each run, Pallas kernels for 19% -> 22%
where the time goes in v2:
time: 431 us; the launch traced here: 429 us
  waiting for transfers between devices  133 us (31%)
  Pallas kernels  131 us (30%)
  starting transfers between devices  55.9 us (13%)
  local copies, waits for them, and re-layouts  42.6 us (10%)
  blocking collectives  26.3 us (6%)
  between operations  16.5 us (4%)
  other arithmetic  12.9 us (3%)
  matrix products  10.2 us (2%)
    pallas_call x5, Pallas kernels, inverted(): pl.pallas_call(functools.partial(inverse_kernel, size), out_shape=(jax.Sh...  118 us
    ppermute x19, waiting for transfers between devices, shifted(): return lax.ppermute(block, axis, route)  80.6 us
    ppermute x19, starting transfers between devices, shifted(): return lax.ppermute(block, axis, route)  55.4 us
    all_gather x13, waiting for transfers between devices, gathered(): return lax.all_gather(part, 'rows', axis=0, tiled=True)  52 us
    unnamed x104, local copies, waits for them, and re-layouts  27.5 us
    all_gather x5, blocking collectives, gathered(): return lax.all_gather(part, 'rows', axis=0, tiled=True)  26.3 us
    pallas_call x4, Pallas kernels, updates(): pl.pallas_call(functools.partial(updates_kernel, rows), out_shape=(messag...  13.6 us
    dot_general x13, matrix products, product(): return jnp.dot(left_part, right_part, precision=HIGHEST)  10.2 us
  transfers between devices with their start and end apart: 32, of which 20 were waited for; matrix products, arithmetic and copies ran while one was open for 6% of the time, Pallas kernels for 22%

profile of v2, /device:TPU:0, one launch (start us, length us, event | category | flops | bytes accessed | tf_op | source)
XLA Modules:
  0.0 428.8 jit_solution(2039204875611681799)
XLA Ops:
  11.5 6.0 %all-gather.3 = f32[1,512]{1,0:T(1,128)S(1)} all-gather(f32[1,128]{1,0:T(1,128)S(1)} %get-tuple-element.50), channel_id=5, replica_groups=mesh['tm'=8,'rows'=4] {'rows'}, dimensions={1}, use_global_device_ids=true | all-gather | bytes 2560 | tf_op jit(solution)/shard_map/all_gather | solution.py:184
  17.5 11.6 %all-gather.46.cloned.1.call-done = f32[1,512,512]{2,1,0:T(8,128)} async-done(((f32[1,128,512]{2,1,0:T(8,128)}), f32[1,512,512]{2,1,0:T(8,128)}) %all-gather.46.cloned.1.call-update) | async-done | bytes 1048592 | tf_op jit(solution)/shard_map/all_gather | solution.py:184
  30.2 17.2 %all-gather.42.cloned.1.call-done = f32[1,512,512]{2,1,0:T(8,128)} async-done(((f32[1,128,512]{2,1,0:T(8,128)}), f32[1,512,512]{2,1,0:T(8,128)}) %all-gather.42.cloned.1.call-update) | async-done | bytes 1048592 | tf_op jit(solution)/shard_map/all_gather | solution.py:184
  48.6 23.5 %shard_map.50 = (f32[512,512]{1,0:T(8,128)S(1)}, f32[8,128]{1,0:T(8,128)S(1)}) custom-call(f32[512,512]{1,0:T(8,128)S(1)} %bitcast.85), custom_call_target="tpu_custom_call" | custom-call | flops 10737418240 | bytes 2097152 | tf_op jit(solution)/shard_map/pallas_call | solution.py:106
  81.1 6.3 %collective-permute-done = f32[136,512]{1,0:T(8,128)S(1)} collective-permute-done((f32[136,512]{1,0:T(8,128)S(1)}, f32[136,512]{1,0:T(8,128)S(1)}, u32[]{:S(2)}, u32[]{:S(2)}) %collective-permute-start) | collective-permute-done | bytes 278560 | tf_op jit(solution)/shard_map/ppermute | solution.py:166
  93.3 5.1 %collective-permute-done.1 = f32[128,512]{1,0:T(8,128)S(1)} collective-permute-done((f32[128,512]{1,0:T(8,128)S(1)}, f32[128,512]{1,0:T(8,128)S(1)}, u32[]{:S(2)}, u32[]{:S(2)}) %collective-permute-start.1) | collective-permute-done | bytes 262176 | tf_op jit(solution)/shard_map/ppermute | solution.py:166
  99.9 5.2 %all-gather.4 = f32[1,512]{1,0:T(1,128)S(1)} all-gather(f32[1,128]{1,0:T(1,128)S(1)} %slice.158), channel_id=6, replica_groups=mesh['tm'=8,'rows'=4] {'rows'}, dimensions={1}, use_global_device_ids=true | all-gather | bytes 2560 | tf_op jit(solution)/shard_map/all_gather | solution.py:184
  114.0 23.5 %shard_map.52 = (f32[512,512]{1,0:T(8,128)S(1)}, f32[8,128]{1,0:T(8,128)S(1)}) custom-call(f32[512,512]{1,0:T(8,128)S(1)} %copy-done.22), custom_call_target="tpu_custom_call" | custom-call | flops 10737418240 | bytes 2097152 | tf_op jit(solution)/shard_map/pallas_call | solution.py:106
  147.8 9.0 %collective-permute-done.5 = f32[128,512]{0,1:T(8,128)S(1)} collective-permute-done((f32[128,512]{0,1:T(8,128)S(1)}, f32[128,512]{0,1:T(8,128)S(1)}, u32[]{:S(2)}, u32[]{:S(2)}) %collective-permute-start.5) | collective-permute-done | bytes 262176 | tf_op jit(solution)/shard_map/ppermute | solution.py:166
  159.0 4.9 %collective-permute-start.3 = (f32[136,512]{1,0:T(8,128)S(1)}, f32[136,512]{1,0:T(8,128)S(1)}, u32[]{:S(2)}, u32[]{:S(2)}) collective-permute-start(f32[136,512]{1,0:T(8,128)S(1)} %copy-done.27), channel_id=1, source_target_pairs={{0,4},{4,8},{8,12},{12,16},{16,20},{20,24},{24,28},{1,5},{5,9},{9,... | collective-permute-start | bytes 835592 | tf_op jit(solution)/shard_map/ppermute | solution.py:166
  168.2 6.1 %collective-permute-done.3 = f32[136,512]{1,0:T(8,128)S(1)} collective-permute-done((f32[136,512]{1,0:T(8,128)S(1)}, f32[136,512]{1,0:T(8,128)S(1)}, u32[]{:S(2)}, u32[]{:S(2)}) %collective-permute-start.3) | collective-permute-done | bytes 278560 | tf_op jit(solution)/shard_map/ppermute | solution.py:166
  180.5 5.7 %collective-permute-done.4 = f32[128,512]{1,0:T(8,128)S(1)} collective-permute-done((f32[128,512]{1,0:T(8,128)S(1)}, f32[128,512]{1,0:T(8,128)S(1)}, u32[]{:S(2)}, u32[]{:S(2)}) %collective-permute-start.4) | collective-permute-done | bytes 262176 | tf_op jit(solution)/shard_map/ppermute | solution.py:166
  187.0 5.0 %all-gather.5 = f32[1,512]{1,0:T(1,128)S(1)} all-gather(f32[1,128]{1,0:T(1,128)S(1)} %slice.163), channel_id=7, replica_groups=mesh['tm'=8,'rows'=4] {'rows'}, dimensions={1}, use_global_device_ids=true | all-gather | bytes 2560 | tf_op jit(solution)/shard_map/all_gather | solution.py:184
  197.7 23.5 %shard_map.54 = (f32[512,512]{1,0:T(8,128)S(1)}, f32[8,128]{1,0:T(8,128)S(1)}) custom-call(f32[512,512]{1,0:T(8,128)S(1)} %copy-done.23), custom_call_target="tpu_custom_call" | custom-call | flops 10737418240 | bytes 2097152 | tf_op jit(solution)/shard_map/pallas_call | solution.py:106
  231.7 9.6 %collective-permute-done.9 = f32[128,512]{0,1:T(8,128)S(1)} collective-permute-done((f32[128,512]{0,1:T(8,128)S(1)}, f32[128,512]{0,1:T(8,128)S(1)}, u32[]{:S(2)}, u32[]{:S(2)}) %collective-permute-start.9) | collective-permute-done | bytes 262176 | tf_op jit(solution)/shard_map/ppermute | solution.py:166
  243.4 4.6 %collective-permute-start.7 = (f32[136,512]{1,0:T(8,128)S(1)}, f32[136,512]{1,0:T(8,128)S(1)}, u32[]{:S(2)}, u32[]{:S(2)}) collective-permute-start(f32[136,512]{1,0:T(8,128)S(1)} %copy-done.29), channel_id=1, source_target_pairs={{0,8},{4,12},{8,16},{12,20},{16,24},{20,28},{1,9},{5,13},{9,17},{1... | collective-permute-start | bytes 835592 | tf_op jit(solution)/shard_map/ppermute | solution.py:166
  266.4 5.0 %all-gather.6 = f32[1,512]{1,0:T(1,128)S(1)} all-gather(f32[1,128]{1,0:T(1,128)S(1)} %slice.168), channel_id=8, replica_groups=mesh['tm'=8,'rows'=4] {'rows'}, dimensions={1}, use_global_device_ids=true | all-gather | bytes 2560 | tf_op jit(solution)/shard_map/all_gather | solution.py:184
  277.9 23.5 %shard_map.56 = (f32[512,512]{1,0:T(8,128)S(1)}, f32[8,128]{1,0:T(8,128)S(1)}) custom-call(f32[512,512]{1,0:T(8,128)S(1)} %copy-done.24), custom_call_target="tpu_custom_call" | custom-call | flops 10737418240 | bytes 2097152 | tf_op jit(solution)/shard_map/pallas_call | solution.py:106
  310.2 5.5 %collective-permute-start.11 = (f32[136,512]{1,0:T(8,128)S(1)}, f32[136,512]{1,0:T(8,128)S(1)}, u32[]{:S(2)}, u32[]{:S(2)}) collective-permute-start(f32[136,512]{1,0:T(8,128)S(1)} %get-tuple-element.41), channel_id=1, source_target_pairs={{0,16},{4,20},{8,24},{12,28},{1,17},{5,21},{9,25},{13,29},{2,18},{... | collective-permute-start | bytes 835592 | tf_op jit(solution)/shard_map/ppermute | solution.py:166
  315.7 10.8 %collective-permute-done.10 = f32[136,512]{1,0:T(8,128)S(1)} collective-permute-done((f32[136,512]{1,0:T(8,128)S(1)}, f32[136,512]{1,0:T(8,128)S(1)}, u32[]{:S(2)}, u32[]{:S(2)}) %collective-permute-start.10) | collective-permute-done | bytes 278560 | tf_op jit(solution)/shard_map/ppermute | solution.py:166
  327.3 19.0 %all-gather.40.cloned.1.call-done.matrix_ref = f32[512,512]{1,0:T(8,128)} async-done(((f32[128,512]{1,0:T(8,128)}), f32[512,512]{1,0:T(8,128)}) %all-gather.40.cloned.1.call-update) | async-done | bytes 1048592 | tf_op jit(solution)/shard_map/all_gather | solution.py:184
  347.6 23.5 %shard_map.58 = (f32[512,512]{1,0:T(8,128)S(1)}, f32[8,128]{1,0:T(8,128)S(1)}) custom-call(f32[512,512]{1,0:T(8,128)S(1)} %copy-done.25), custom_call_target="tpu_custom_call" | custom-call | flops 10737418240 | bytes 2097152 | tf_op jit(solution)/shard_map/pallas_call | solution.py:106
  371.7 5.0 %all-gather.7 = f32[1,512]{1,0:T(1,128)S(1)} all-gather(f32[1,128]{1,0:T(1,128)S(1)} %get-tuple-element.48), channel_id=9, replica_groups=mesh['tm'=8,'rows'=4] {'rows'}, dimensions={1}, use_global_device_ids=true | all-gather | bytes 2560 | tf_op jit(solution)/shard_map/all_gather | solution.py:184
  384.8 4.5 %collective-permute-done.13 = f32[640]{0:T(1024)S(1)} collective-permute-done((f32[640]{0:T(1024)S(1)}, f32[640]{0:T(1024)S(1)}, u32[]{:S(2)}, u32[]{:S(2)}) %collective-permute-start.13) | collective-permute-done | bytes 2592 | tf_op jit(solution)/shard_map/ppermute | solution.py:166
  (241 shorter events, 148.7 us)
Async XLA Ops:
  7.2 21.9 %all-gather.46.cloned.1.call-start = ((), (), s32[]{:S(2)}) async-start(), calls=%async_computation.12 | async-start | bytes 1310720 | tf_op jit(solution)/shard_map/all_gather | solution.py:184
  9.2 38.1 %all-gather.42.cloned.1.call-start = ((), (), s32[]{:S(2)}) async-start(), calls=%async_computation.10 | async-start | bytes 1310720 | tf_op jit(solution)/shard_map/all_gather | solution.py:184
  10.0 62.1 %all-gather.44.cloned.1.call-start = ((), (), s32[]{:S(2)}) async-start(), calls=%async_computation.11 | async-start | bytes 1310720 | tf_op jit(solution)/shard_map/all_gather | solution.py:184
  10.8 94.3 %all-gather.26.cloned.1.call-start = ((), (), s32[]{:S(2)}) async-start(), calls=%async_computation.2 | async-start | bytes 1310720 | tf_op jit(solution)/shard_map/all_gather | solution.py:184
  77.6 35.2 %all-gather.22.cloned.1.call-start = ((), (), s32[]{:S(2)}) async-start(), calls=%async_computation | async-start | bytes 1310720 | tf_op jit(solution)/shard_map/all_gather | solution.py:184
  77.7 9.7 %collective-permute-start = (f32[136,512]{1,0:T(8,128)S(1)}, f32[136,512]{1,0:T(8,128)S(1)}, u32[]{:S(2)}, u32[]{:S(2)}) collective-permute-start(f32[136,512]{1,0:T(8,128)S(1)} %get-tuple-element.26), channel_id=1, source_target_pairs={{0,4},{4,8},{8,12},{12,16},{16,20},{20,24},{24,28},{1,5},{5,9},{9,... | collective-permute-start | bytes 835592 | tf_op jit(solution)/shard_map/ppermute | solution.py:166
  88.8 48.7 %all-gather.24.cloned.1.call-start = ((), (), s32[]{:S(2)}) async-start(), calls=%async_computation.1 | async-start | bytes 1310720 | tf_op jit(solution)/shard_map/all_gather | solution.py:184
  88.9 9.5 %collective-permute-start.1 = (f32[128,512]{1,0:T(8,128)S(1)}, f32[128,512]{1,0:T(8,128)S(1)}, u32[]{:S(2)}, u32[]{:S(2)}) collective-permute-start(f32[128,512]{1,0:T(8,128)S(1)} %get-tuple-element.28), channel_id=1, source_target_pairs={{0,4},{4,8},{8,12},{12,16},{16,20},{20,24},{24,28},{1,5},{5,9},{9,... | collective-permute-start | bytes 786440 | tf_op jit(solution)/shard_map/ppermute | solution.py:166
  99.1 92.9 %all-gather.32.cloned.1.call-start = ((), (), s32[]{:S(2)}) async-start(), calls=%async_computation.5 | async-start | bytes 1310720 | tf_op jit(solution)/shard_map/all_gather | solution.py:184
  146.4 10.5 %collective-permute-start.5 = (f32[128,512]{0,1:T(8,128)S(1)}, f32[128,512]{0,1:T(8,128)S(1)}, u32[]{:S(2)}, u32[]{:S(2)}) collective-permute-start(f32[128,512]{0,1:T(8,128)S(1)} %copy.8), channel_id=1, source_target_pairs={{4,0},{8,4},{12,8},{16,12},{20,16},{24,20},{28,24},{5,1},{9,5},{13... | collective-permute-start | bytes 786440 | tf_op jit(solution)/shard_map/ppermute | solution.py:166
  157.6 38.8 %all-gather.28.cloned.1.call-start = ((), (), s32[]{:S(2)}) async-start(), calls=%async_computation.3 | async-start | bytes 1310720 | tf_op jit(solution)/shard_map/all_gather | solution.py:184
  157.7 10.5 %collective-permute-start.2 = (f32[136,512]{1,0:T(8,128)S(1)}, f32[136,512]{1,0:T(8,128)S(1)}, u32[]{:S(2)}, u32[]{:S(2)}) collective-permute-start(f32[136,512]{1,0:T(8,128)S(1)} %copy-done.31), channel_id=1, source_target_pairs={{4,0},{8,4},{12,8},{16,12},{20,16},{24,20},{28,24},{5,1},{9,5},{13... | collective-permute-start | bytes 835592 | tf_op jit(solution)/shard_map/ppermute | solution.py:166
  159.0 15.3 %collective-permute-start.3 = (f32[136,512]{1,0:T(8,128)S(1)}, f32[136,512]{1,0:T(8,128)S(1)}, u32[]{:S(2)}, u32[]{:S(2)}) collective-permute-start(f32[136,512]{1,0:T(8,128)S(1)} %copy-done.27), channel_id=1, source_target_pairs={{0,4},{4,8},{8,12},{12,16},{16,20},{20,24},{24,28},{1,5},{5,9},{9,... | collective-permute-start | bytes 835592 | tf_op jit(solution)/shard_map/ppermute | solution.py:166
  176.0 45.2 %all-gather.30.cloned.1.call-start = ((), (), s32[]{:S(2)}) async-start(), calls=%async_computation.4 | async-start | bytes 1310720 | tf_op jit(solution)/shard_map/all_gather | solution.py:184
  176.1 10.1 %collective-permute-start.4 = (f32[128,512]{1,0:T(8,128)S(1)}, f32[128,512]{1,0:T(8,128)S(1)}, u32[]{:S(2)}, u32[]{:S(2)}) collective-permute-start(f32[128,512]{1,0:T(8,128)S(1)} %get-tuple-element.33), channel_id=1, source_target_pairs={{0,4},{4,8},{8,12},{12,16},{16,20},{20,24},{24,28},{1,5},{5,9},{9,... | collective-permute-start | bytes 786440 | tf_op jit(solution)/shard_map/ppermute | solution.py:166
  186.9 84.5 %all-gather.38.cloned.1.call-start = ((), (), s32[]{:S(2)}) async-start(), calls=%async_computation.8 | async-start | bytes 1310720 | tf_op jit(solution)/shard_map/all_gather | solution.py:184
  230.0 11.3 %collective-permute-start.9 = (f32[128,512]{0,1:T(8,128)S(1)}, f32[128,512]{0,1:T(8,128)S(1)}, u32[]{:S(2)}, u32[]{:S(2)}) collective-permute-start(f32[128,512]{0,1:T(8,128)S(1)} %copy.10), channel_id=1, source_target_pairs={{8,0},{12,4},{16,8},{20,12},{24,16},{28,20},{9,1},{13,5},{17,9},{2... | collective-permute-start | bytes 786440 | tf_op jit(solution)/shard_map/ppermute | solution.py:166
  242.0 34.7 %all-gather.34.cloned.1.call-start = ((), (), s32[]{:S(2)}) async-start(), calls=%async_computation.6 | async-start | bytes 1310720 | tf_op jit(solution)/shard_map/all_gather | solution.py:184
  242.1 10.3 %collective-permute-start.6 = (f32[136,512]{1,0:T(8,128)S(1)}, f32[136,512]{1,0:T(8,128)S(1)}, u32[]{:S(2)}, u32[]{:S(2)}) collective-permute-start(f32[136,512]{1,0:T(8,128)S(1)} %copy-done.33), channel_id=1, source_target_pairs={{8,0},{12,4},{16,8},{20,12},{24,16},{28,20},{9,1},{13,5},{17,9},{2... | collective-permute-start | bytes 835592 | tf_op jit(solution)/shard_map/ppermute | solution.py:166
  243.4 10.1 %collective-permute-start.7 = (f32[136,512]{1,0:T(8,128)S(1)}, f32[136,512]{1,0:T(8,128)S(1)}, u32[]{:S(2)}, u32[]{:S(2)}) collective-permute-start(f32[136,512]{1,0:T(8,128)S(1)} %copy-done.29), channel_id=1, source_target_pairs={{0,8},{4,12},{8,16},{12,20},{16,24},{20,28},{1,9},{5,13},{9,17},{1... | collective-permute-start | bytes 835592 | tf_op jit(solution)/shard_map/ppermute | solution.py:166
  256.0 45.5 %all-gather.36.cloned.1.call-start = ((), (), s32[]{:S(2)}) async-start(), calls=%async_computation.7 | async-start | bytes 1310720 | tf_op jit(solution)/shard_map/all_gather | solution.py:184
  265.6 80.8 %all-gather.40.cloned.1.call-start = ((), (), s32[]{:S(2)}) async-start(), calls=%async_computation.9 | async-start | bytes 1310720 | tf_op jit(solution)/shard_map/all_gather | solution.py:184
  309.0 17.5 %collective-permute-start.10 = (f32[136,512]{1,0:T(8,128)S(1)}, f32[136,512]{1,0:T(8,128)S(1)}, u32[]{:S(2)}, u32[]{:S(2)}) collective-permute-start(f32[136,512]{1,0:T(8,128)S(1)} %get-tuple-element.40), channel_id=1, source_target_pairs={{16,0},{20,4},{24,8},{28,12},{17,1},{21,5},{25,9},{29,13},{18,2},{... | collective-permute-start | bytes 835592 | tf_op jit(solution)/shard_map/ppermute | solution.py:166
  310.2 16.3 %collective-permute-start.11 = (f32[136,512]{1,0:T(8,128)S(1)}, f32[136,512]{1,0:T(8,128)S(1)}, u32[]{:S(2)}, u32[]{:S(2)}) collective-permute-start(f32[136,512]{1,0:T(8,128)S(1)} %get-tuple-element.41), channel_id=1, source_target_pairs={{0,16},{4,20},{8,24},{12,28},{1,17},{5,21},{9,25},{13,29},{2,18},{... | collective-permute-start | bytes 835592 | tf_op jit(solution)/shard_map/ppermute | solution.py:166
  (60 other events, 272.5 us)
Sparse Core Ops, SparseCore 0:
  9.6 19.4 all-gather.45
  30.6 16.7 all-gather.41
  48.9 16.7 all-gather.43
  77.8 16.8 all-gather.25
  96.0 16.7 all-gather.21
  114.2 16.7 all-gather.23
  157.7 16.7 all-gather.31
  176.1 16.7 all-gather.27
  194.5 16.7 all-gather.29
  242.1 16.1 all-gather.37
  259.9 16.7 all-gather.33
  278.1 16.7 all-gather.35
  327.4 18.8 all-gather.39

commit v3 on v2

--- a/solution.py
+++ b/solution.py
@@ -156,6 +156,177 @@
     )
 
 
+def exchange_kernel(
+    stride, local_up, count, parts, own_ref, up_ref, down_ref, link_ref,
+    new_ref, diag_ref, tails_ref, left_ref, right_ref,
+    got_up, got_down, got_left, got_right, slots,
+    send_sem, recv_sem, gather_send, gather_recv, forward_send, forward_recv,
+):
+    group, me = lax.axis_index("tm"), lax.axis_index("rows")
+    rows = link_ref.shape[0]
+    below = lax.rem(group + count - stride, count)
+    above = lax.rem(group + stride, count)
+    partner = me + 1 - 2 * lax.rem(me, 2)
+
+    barrier = pltpu.get_barrier_semaphore()
+    for other in (below, above):
+        pl.semaphore_signal(
+            barrier, inc=1, device_id={"tm": other}, device_id_type=pl.DeviceIdType.MESH
+        )
+    for distance in range(1, parts):
+        pl.semaphore_signal(
+            barrier, inc=1, device_id={"rows": lax.rem(me + distance, parts)},
+            device_id_type=pl.DeviceIdType.MESH,
+        )
+    pl.semaphore_wait(barrier, parts + 1)
+
+    if local_up:
+        sends_down, gets_down = group < count - 1, group > 0
+    else:
+        place = lax.rem(group, 2 * stride)
+        gets_up, sends_up = place == 0, place == stride
+        sends_down = jnp.logical_and(place == stride, group + stride < count)
+        gets_down = jnp.logical_and(place == 0, group > 0)
+
+    def over_time(source, target, number, other):
+        return pltpu.make_async_remote_copy(
+            src_ref=source, dst_ref=target, send_sem=send_sem.at[number],
+            recv_sem=recv_sem.at[number], device_id={"tm": other},
+            device_id_type=pl.DeviceIdType.MESH,
+        )
+
+    up = over_time(up_ref, got_up, 0, below)
+    down = over_time(down_ref, got_down, 1, above)
+    link_up = over_time(link_ref, got_right, 2, below)
+    link_down = over_time(link_ref, got_left, 3, above)
+
+    if not local_up:
+        @pl.when(sends_up)
+        def _():
+            up.start()
+
+    @pl.when(sends_down)
+    def _():
+        down.start()
+
+    if not local_up:
+        @pl.when(sends_up)
+        def _():
+            link_up.start()
+
+    @pl.when(sends_down)
+    def _():
+        link_down.start()
+
+    if local_up:
+        new_ref[...] = own_ref[...] - up_ref[...]
+    else:
+        new_ref[...] = own_ref[...]
+
+        @pl.when(gets_up)
+        def _():
+            up.wait_recv()
+            new_ref[...] -= got_up[...]
+
+    @pl.when(gets_down)
+    def _():
+        down.wait_recv()
+        new_ref[...] -= got_down[...]
+
+    def over_rows(source, slot, target, send, recv):
+        return pltpu.make_async_remote_copy(
+            src_ref=source, dst_ref=slots.at[slot], send_sem=send, recv_sem=recv,
+            device_id={"rows": target}, device_id_type=pl.DeviceIdType.MESH,
+        )
+
+    chips = parts // 2
+    sent = []
+    for d in range(1, chips):
+        target = lax.rem(me + 2 * d, parts)
+        copy = over_rows(new_ref, me, target, gather_send.at[d], gather_recv.at[d])
+        copy.start()
+        sent.append(copy)
+    forwards = [over_rows(new_ref, me, partner, forward_send.at[0], forward_recv.at[0])]
+    forwards[0].start()
+    slots[me] = new_ref[...]
+    for d in range(1, chips):
+        sent[d - 1].wait_recv()
+        source = lax.rem(me + parts - 2 * d, parts)
+        copy = over_rows(
+            slots.at[source], source, partner, forward_send.at[d], forward_recv.at[d]
+        )
+        copy.start()
+        forwards.append(copy)
+    for copy in forwards:
+        copy.wait_recv()
+    for copy in sent + forwards:
+        copy.wait_send()
+    for part in range(parts):
+        diag_ref[part * rows:(part + 1) * rows, :] = slots[part, 0:rows, :]
+        tails_ref[part * 8:(part + 1) * 8, :] = slots[part, rows:, :]
+
+    left_ref[...] = jnp.zeros(left_ref.shape, jnp.float32)
+
+    @pl.when(gets_down)
+    def _():
+        link_down.wait_recv()
+        left_ref[...] = got_left[...]
+
+    if local_up:
+        right_ref[...] = link_ref[...]
+    else:
+        right_ref[...] = jnp.zeros(right_ref.shape, jnp.float32)
+
+        @pl.when(gets_up)
+        def _():
+            link_up.wait_recv()
+            right_ref[...] = got_right[...]
+
+        @pl.when(sends_up)
+        def _():
+            up.wait_send()
+            link_up.wait_send()
+
+    @pl.when(sends_down)
+    def _():
+        down.wait_send()
+        link_down.wait_send()
+
+
+def exchanged(number, stride, local_up, own, up, down, link):
+    rows, size = link.shape
+    count, parts = lax.axis_size("tm"), lax.axis_size("rows")
+    message = jax.ShapeDtypeStruct((rows + 8, size), jnp.float32)
+    part = jax.ShapeDtypeStruct((rows, size), jnp.float32)
+    new, diag, tails, left, right = pl.pallas_call(
+        functools.partial(exchange_kernel, stride, local_up, count, parts),
+        out_shape=(
+            message, jax.ShapeDtypeStruct((size, size), jnp.float32),
+            jax.ShapeDtypeStruct((8 * parts, size), jnp.float32), part, part,
+        ),
+        in_specs=[pl.BlockSpec(memory_space=pltpu.VMEM)] * 4,
+        out_specs=(pl.BlockSpec(memory_space=pltpu.VMEM),) * 5,
+        scratch_shapes=[
+            pltpu.VMEM((rows + 8, size), jnp.float32),
+            pltpu.VMEM((rows + 8, size), jnp.float32),
+            pltpu.VMEM((rows, size), jnp.float32),
+            pltpu.VMEM((rows, size), jnp.float32),
+            pltpu.VMEM((parts, rows + 8, size), jnp.float32),
+            pltpu.SemaphoreType.DMA((4,)),
+            pltpu.SemaphoreType.DMA((4,)),
+            pltpu.SemaphoreType.DMA((parts // 2,)),
+            pltpu.SemaphoreType.DMA((parts // 2,)),
+            pltpu.SemaphoreType.DMA((parts // 2,)),
+            pltpu.SemaphoreType.DMA((parts // 2,)),
+        ],
+        compiler_params=pltpu.CompilerParams(
+            collective_id=number, has_side_effects=True, vmem_limit_bytes=24 << 20
+        ),
+    )(own, up, down, link)
+    vector = tails.reshape(parts, 8, size)[:, 0, :rows].reshape(size)
+    return new, diag, vector, left, right
+
+
 def product(left_part, right_part):
     return jnp.dot(left_part, right_part, precision=HIGHEST)
 
@@ -186,36 +357,31 @@
     def as_row(vector):
         return jnp.pad(vector[None], ((0, 7), (0, size - rows)))
 
-    def eliminated(diag_part, left_part, right_part, vector_part, tail):
-        diag = gathered(diag_part)
-        left, right, vector = gathered(left_part), gathered(right_part), gathered(vector_part)
+    def eliminated(diag, vector, left_part, right_part, tail):
+        left, right = gathered(left_part), gathered(right_part)
         inverse, logs = inverted(diag)
         up, down, link = updates(
             inverse, left, right, left_part, my_columns_t(right), vector, logs, tail
         )
         return up, down, link, (inverse, left, right, vector)
 
-    tail = jnp.zeros((8, size), jnp.float32)
     up, down, link, chain = eliminated(
-        diag_blocks[1], coupling[0], coupling[1] * not_last, rhs[1], tail
+        gathered(diag_blocks[1]), gathered(rhs[1]), coupling[0], coupling[1] * not_last,
+        jnp.zeros((8, size), jnp.float32),
     )
-    down = shifted(down, "tm", 1)
-    left, right = shifted(link, "tm", 1), link
-    diag = diag_blocks[0] - up[:rows] - down[:rows]
-    tail = as_row(rhs[0]) - up[rows:] - down[rows:]
+    own = jnp.concatenate([diag_blocks[0], as_row(rhs[0])])
+    own, diag, vector, left, right = exchanged(0, 1, True, own, up, down, link)
     levels_kept = []
     for level_index in range(level_count):
         stride = 1 << level_index
         is_pivot = group_index % (2 * stride) == stride
-        up, down, link, kept = eliminated(diag, left, right, tail[0, :rows], tail)
+        up, down, link, kept = eliminated(diag, vector, left, right, own[rows:])
         levels_kept.append((is_pivot, kept))
-        up, down = shifted(up, "tm", -stride), shifted(down, "tm", stride)
-        diag = diag - up[:rows] - down[:rows]
-        tail = tail - up[rows:] - down[rows:]
-        if level_index < level_count - 1:
-            left, right = shifted(link, "tm", stride), shifted(link, "tm", -stride)
-    vector = gathered(tail[0, :rows])
-    inverse, logs = inverted(gathered(diag))
+        own, diag, vector, left, right = exchanged(
+            level_index + 1, stride, False, own, up, down, link
+        )
+    tail = own[rows:]
+    inverse, logs = inverted(diag)
     total = jnp.sum(logs[0] - tail[0, size - TILE:])
     states = jnp.concatenate([product(inverse, vector), jnp.full((TILE,), total)])
     for level_index in reversed(range(level_count)):

time: 431 us -> 379 us (0.88)
  Pallas kernels: 131 us -> 207 us
  waiting for transfers between devices: 133 us -> 64.8 us
  starting transfers between devices: 55.9 us -> 10.2 us
  blocking collectives: 26.3 us -> 5.96 us
  local copies, waits for them, and re-layouts: 42.6 us -> 48.8 us
    pallas_call x0 -> x4, Pallas kernels: none -> 75.9 us  [exchanged(): pl.pallas_call(functools.partial(exchange_kernel, stride, local_up, count...]
    ppermute x19 -> x7, waiting for transfers between devices: 80.6 us -> 12.4 us  [shifted(): return lax.ppermute(block, axis, route)]
    ppermute x19 -> x7, starting transfers between devices: 55.4 us -> 9.69 us  [shifted(): return lax.ppermute(block, axis, route)]
    all_gather x5 -> x1, blocking collectives: 26.3 us -> 5.96 us  [gathered(): return lax.all_gather(part, 'rows', axis=0, tiled=True)]
    sub x8 -> x0, other arithmetic: 6.43 us -> none  [the longest x3 4.18 us: local(): diag = diag - up[:rows] - down[:rows]]
    pallas_call x3, local copies, waits for them, and re-layouts: 1.13 us -> 5.51 us  [exchanged(): pl.pallas_call(functools.partial(exchange_kernel, stride, local_up, count...]
    all_gather x13 -> x9, waiting for transfers between devices: 52 us -> 49.8 us  [gathered(): return lax.all_gather(part, 'rows', axis=0, tiled=True)]
    unnamed x104 -> x80, local copies, waits for them, and re-layouts: 27.5 us -> 29.4 us
  transfers between devices with their start and end apart: 32 -> 16, of which waited for: 20 -> 10; matrix products, arithmetic and copies ran while one was open for 6% -> 7% of each run, Pallas kernels for 22% -> 25%
where the time goes in v3:
time: 379 us; the launch traced here: 377 us
  Pallas kernels  207 us (55%)
  waiting for transfers between devices  64.8 us (17%)
  local copies, waits for them, and re-layouts  48.8 us (13%)
  between operations  16.2 us (4%)
  matrix products  14.1 us (4%)
  starting transfers between devices  10.2 us (3%)
  other arithmetic  10.1 us (3%)
  blocking collectives  5.96 us (2%)
    pallas_call x5, Pallas kernels, inverted(): pl.pallas_call(functools.partial(inverse_kernel, size), out_shape=(jax.Sh...  118 us
    pallas_call x4, Pallas kernels, exchanged(): pl.pallas_call(functools.partial(exchange_kernel, stride, local_up, count...  75.9 us
    all_gather x9, waiting for transfers between devices, gathered(): return lax.all_gather(part, 'rows', axis=0, tiled=True)  49.8 us
    unnamed x80, local copies, waits for them, and re-layouts  29.4 us
    dot_general x13, matrix products, product(): return jnp.dot(left_part, right_part, precision=HIGHEST)  14.1 us
    pallas_call x4, Pallas kernels, updates(): pl.pallas_call(functools.partial(updates_kernel, rows), out_shape=(messag...  13.3 us
    ppermute x7, waiting for transfers between devices, shifted(): return lax.ppermute(block, axis, route)  12.4 us
    ppermute x7, starting transfers between devices, shifted(): return lax.ppermute(block, axis, route)  9.69 us
  transfers between devices with their start and end apart: 16, of which 10 were waited for; matrix products, arithmetic and copies ran while one was open for 7% of the time, Pallas kernels for 25%

profile of v3, /device:TPU:0, one launch (start us, length us, event | category | flops | bytes accessed | tf_op | source)
XLA Modules:
  0.0 377.0 jit_solution(7020947670839417418)
XLA Ops:
  11.5 6.0 %all-gather.3 = f32[1,512]{1,0:T(1,128)S(1)} all-gather(f32[1,128]{1,0:T(1,128)S(1)} %get-tuple-element.87), channel_id=5, replica_groups=mesh['tm'=8,'rows'=4] {'rows'}, dimensions={1}, use_global_device_ids=true | all-gather | bytes 2560 | tf_op jit(solution)/shard_map/all_gather | solution.py:355
  17.5 11.5 %all-gather.30.cloned.1.call-done = f32[1,512,512]{2,1,0:T(8,128)} async-done(((f32[1,128,512]{2,1,0:T(8,128)}), f32[1,512,512]{2,1,0:T(8,128)}) %all-gather.30.cloned.1.call-update) | async-done | bytes 1048592 | tf_op jit(solution)/shard_map/all_gather | solution.py:355
  31.0 16.4 %all-gather.26.cloned.1.call-done = f32[1,512,512]{2,1,0:T(8,128)} async-done(((f32[1,128,512]{2,1,0:T(8,128)}), f32[1,512,512]{2,1,0:T(8,128)}) %all-gather.26.cloned.1.call-update) | async-done | bytes 1048592 | tf_op jit(solution)/shard_map/all_gather | solution.py:355
  48.6 23.5 %shard_map.50 = (f32[512,512]{1,0:T(8,128)S(1)}, f32[8,128]{1,0:T(8,128)S(1)}) custom-call(f32[512,512]{1,0:T(8,128)S(1)} %bitcast.92), custom_call_target="tpu_custom_call" | custom-call | flops 10737418240 | bytes 2097152 | tf_op jit(solution)/shard_map/pallas_call | solution.py:106
  74.4 3.3 shard_map.51
  77.7 17.1 %shard_map.52 = (f32[136,512]{1,0:T(8,128)S(1)}, f32[512,512]{1,0:T(8,128)S(1)}, f32[32,512]{1,0:T(8,128)S(1)}, f32[128,512]{1,0:T(8,128)}, f32[128,512]{1,0:T(8,128)S(1)}) custom-call(f32[136,512]{1,0:T(8,128)S(1)} %select_maximum_fusion.own_ref, f32[136,512]{1,0:T(8,128)S(1)} %get-tuple-element.44.up_ref, f32[136,512]{1,0:T(8,128)S(1)} %get-tuple-element.45.down_ref, ...), custom_call_target="tpu_custom_call" | custom-call | tf_op jit(solution)/shard_map/pallas_call | solution.py:301
  100.4 23.5 %shard_map.53 = (f32[512,512]{1,0:T(8,128)S(1)}, f32[8,128]{1,0:T(8,128)S(1)}) custom-call(f32[512,512]{1,0:T(8,128)S(1)} %copy-done.30), custom_call_target="tpu_custom_call" | custom-call | flops 10737418240 | bytes 2097152 | tf_op jit(solution)/shard_map/pallas_call | solution.py:106
  123.9 2.6 copy.7.right_ref
  129.3 5.8 %all-gather.14.cloned.1.call-done.left_ref = f32[512,512]{1,0:T(8,128)} async-done(((f32[128,512]{1,0:T(8,128)}), f32[512,512]{1,0:T(8,128)}) %all-gather.14.cloned.1.call-update) | async-done | bytes 1048592 | tf_op jit(solution)/shard_map/all_gather | solution.py:355
  138.6 3.3 shard_map.54
  141.9 19.2 %shard_map.55 = (f32[136,512]{1,0:T(8,128)S(1)}, f32[512,512]{1,0:T(8,128)S(1)}, f32[32,512]{1,0:T(8,128)S(1)}, f32[128,512]{1,0:T(8,128)}, f32[128,512]{1,0:T(8,128)S(1)}) custom-call(f32[136,512]{1,0:T(8,128)S(1)} %copy-done.20, f32[136,512]{1,0:T(8,128)S(1)} %get-tuple-element.54.up_ref, f32[136,512]{1,0:T(8,128)S(1)} %get-tuple-element.55.down_ref, ...), custom_call_target="tpu_custom_call" | custom-call | tf_op jit(solution)/shard_map/pallas_call | solution.py:301
  167.5 23.5 %shard_map.56 = (f32[512,512]{1,0:T(8,128)S(1)}, f32[8,128]{1,0:T(8,128)S(1)}) custom-call(f32[512,512]{1,0:T(8,128)S(1)} %copy-done.32), custom_call_target="tpu_custom_call" | custom-call | flops 10737418240 | bytes 2097152 | tf_op jit(solution)/shard_map/pallas_call | solution.py:106
  193.6 2.6 copy.9.right_ref
  199.0 12.9 %all-gather.18.cloned.1.call-done.left_ref = f32[512,512]{1,0:T(8,128)} async-done(((f32[128,512]{1,0:T(8,128)}), f32[512,512]{1,0:T(8,128)}) %all-gather.18.cloned.1.call-update) | async-done | bytes 1048592 | tf_op jit(solution)/shard_map/all_gather | solution.py:355
  216.6 3.3 shard_map.57
  219.9 19.4 %shard_map.58 = (f32[136,512]{1,0:T(8,128)S(1)}, f32[512,512]{1,0:T(8,128)S(1)}, f32[32,512]{1,0:T(8,128)S(1)}, f32[128,512]{1,0:T(8,128)}, f32[128,512]{1,0:T(8,128)S(1)}) custom-call(f32[136,512]{1,0:T(8,128)S(1)} %copy-done.22, f32[136,512]{1,0:T(8,128)S(1)} %get-tuple-element.64.up_ref, f32[136,512]{1,0:T(8,128)S(1)} %get-tuple-element.65.down_ref, ...), custom_call_target="tpu_custom_call" | custom-call | tf_op jit(solution)/shard_map/pallas_call | solution.py:301
  245.7 23.5 %shard_map.59 = (f32[512,512]{1,0:T(8,128)S(1)}, f32[8,128]{1,0:T(8,128)S(1)}) custom-call(f32[512,512]{1,0:T(8,128)S(1)} %copy-done.34), custom_call_target="tpu_custom_call" | custom-call | flops 10737418240 | bytes 2097152 | tf_op jit(solution)/shard_map/pallas_call | solution.py:106
  270.3 2.5 copy.11.right_ref
  281.9 3.3 shard_map.60
  285.2 20.2 %shard_map.61 = (f32[136,512]{1,0:T(8,128)S(1)}, f32[512,512]{1,0:T(8,128)S(1)}, f32[32,512]{1,0:T(8,128)S(1)}, f32[128,512]{1,0:T(8,128)}, f32[128,512]{1,0:T(8,128)}) custom-call(f32[136,512]{1,0:T(8,128)S(1)} %copy-done.24, f32[136,512]{1,0:T(8,128)S(1)} %get-tuple-element.74.up_ref, f32[136,512]{1,0:T(8,128)S(1)} %get-tuple-element.75.down_ref, ...), custom_call_target="tpu_custom_call" | custom-call | tf_op jit(solution)/shard_map/pallas_call | solution.py:301
  305.4 23.5 %shard_map.62 = (f32[512,512]{1,0:T(8,128)S(1)}, f32[8,128]{1,0:T(8,128)S(1)}) custom-call(f32[512,512]{1,0:T(8,128)S(1)} %get-tuple-element.77.matrix_ref), custom_call_target="tpu_custom_call" | custom-call | flops 10737418240 | bytes 2097152 | tf_op jit(solution)/shard_map/pallas_call | solution.py:106
  335.9 3.2 collective-permute-done.1
  354.6 4.0 %collective-permute-done.5 = f32[640]{0:T(1024)S(1)} collective-permute-done((f32[640]{0:T(1024)S(1)}, f32[640]{0:T(1024)S(1)}, u32[]{:S(2)}, u32[]{:S(2)}) %collective-permute-start.5) | collective-permute-done | bytes 2592 | tf_op jit(solution)/shard_map/ppermute | solution.py:337
  363.5 3.2 collective-permute-done.6
  (177 shorter events, 83.3 us)
Async XLA Ops:
  7.2 21.9 %all-gather.30.cloned.1.call-start = ((), (), s32[]{:S(2)}) async-start(), calls=%async_computation.8 | async-start | bytes 1310720 | tf_op jit(solution)/shard_map/all_gather | solution.py:355
  9.2 38.1 %all-gather.26.cloned.1.call-start = ((), (), s32[]{:S(2)}) async-start(), calls=%async_computation.6 | async-start | bytes 1310720 | tf_op jit(solution)/shard_map/all_gather | solution.py:355
  10.1 62.0 %all-gather.28.cloned.1.call-start = ((), (), s32[]{:S(2)}) async-start(), calls=%async_computation.7 | async-start | bytes 1310720 | tf_op jit(solution)/shard_map/all_gather | solution.py:355
  10.8 113.1 %all-gather.16.cloned.1.call-start = ((), (), s32[]{:S(2)}) async-start(), calls=%async_computation.1 | async-start | bytes 1310720 | tf_op jit(solution)/shard_map/all_gather | solution.py:355
  48.6 23.6 %copy-start = (f32[1,512,512]{2,1,0:T(8,128)S(1)}, f32[1,512,512]{2,1,0:T(8,128)}, u32[]{:S(2)}) copy-start(f32[1,512,512]{2,1,0:T(8,128)} %all-gather.30.cloned.1.call-done) | copy-start | bytes 3145732
  96.2 2.9 copy-start.29
  98.2 36.9 %all-gather.14.cloned.1.call-start = ((), (), s32[]{:S(2)}) async-start(), calls=%async_computation | async-start | bytes 1310720 | tf_op jit(solution)/shard_map/all_gather | solution.py:355
  98.8 94.8 %all-gather.20.cloned.1.call-start = ((), (), s32[]{:S(2)}) async-start(), calls=%async_computation.3 | async-start | bytes 1310720 | tf_op jit(solution)/shard_map/all_gather | solution.py:355
  165.4 46.5 %all-gather.18.cloned.1.call-start = ((), (), s32[]{:S(2)}) async-start(), calls=%async_computation.2 | async-start | bytes 1310720 | tf_op jit(solution)/shard_map/all_gather | solution.py:355
  166.1 104.1 %all-gather.24.cloned.1.call-start = ((), (), s32[]{:S(2)}) async-start(), calls=%async_computation.5 | async-start | bytes 1310720 | tf_op jit(solution)/shard_map/all_gather | solution.py:355
  243.5 33.6 %all-gather.22.cloned.1.call-start = ((), (), s32[]{:S(2)}) async-start(), calls=%async_computation.4 | async-start | bytes 1310720 | tf_op jit(solution)/shard_map/all_gather | solution.py:355
  331.2 2.8 collective-permute-start
  332.5 6.6 %copy-start.37 = (f32[512,512]{0,1:T(8,128)S(1)}, f32[512,512]{0,1:T(8,128)}, u32[]{:S(2)}) copy-start(f32[512,512]{0,1:T(8,128)} %all-gather.24.cloned.1.call-done) | copy-start | bytes 3145732
  332.5 6.5 %collective-permute-start.1 = (f32[640]{0:T(1024)S(1)}, f32[640]{0:T(1024)S(1)}, u32[]{:S(2)}, u32[]{:S(2)}) collective-permute-start(f32[640]{0:T(1024)S(1)} %concatenate.32), channel_id=1, source_target_pairs={{16,0},{20,4},{24,8},{28,12},{17,1},{21,5},{25,9},{29,13},{18,2},{... | collective-permute-start | bytes 7688 | tf_op jit(solution)/shard_map/ppermute | solution.py:337
  334.0 5.8 %copy-start.10 = (f32[512,512]{1,0:T(8,128)S(1)}, f32[512,512]{1,0:T(8,128)}, u32[]{:S(2)}) copy-start(f32[512,512]{1,0:T(8,128)} %copy-done.8) | copy-start | bytes 3145732
  341.4 3.0 collective-permute-start.2
  342.7 5.6 %copy-start.36 = (f32[512,512]{0,1:T(8,128)S(1)}, f32[512,512]{0,1:T(8,128)}, u32[]{:S(2)}) copy-start(f32[512,512]{0,1:T(8,128)} %all-gather.20.cloned.1.call-done) | copy-start | bytes 3145732
  342.7 5.6 %collective-permute-start.3 = (f32[640]{0:T(1024)S(1)}, f32[640]{0:T(1024)S(1)}, u32[]{:S(2)}, u32[]{:S(2)}) collective-permute-start(f32[640]{0:T(1024)S(1)} %maximum_select_fusion), channel_id=1, source_target_pairs={{8,0},{12,4},{16,8},{20,12},{24,16},{28,20},{9,1},{13,5},{17,9},{2... | collective-permute-start | bytes 7688 | tf_op jit(solution)/shard_map/ppermute | solution.py:337
  344.4 4.6 %copy-start.6 = (f32[512,512]{1,0:T(8,128)S(1)}, f32[512,512]{1,0:T(8,128)}, u32[]{:S(2)}) copy-start(f32[512,512]{1,0:T(8,128)} %copy-done.4) | copy-start | bytes 3145732
  350.0 2.8 collective-permute-start.4
  351.3 7.3 %copy-start.35 = (f32[512,512]{0,1:T(8,128)S(1)}, f32[512,512]{0,1:T(8,128)}, u32[]{:S(2)}) copy-start(f32[512,512]{0,1:T(8,128)} %all-gather.16.cloned.1.call-done) | copy-start | bytes 3145732
  351.3 7.3 %collective-permute-start.5 = (f32[640]{0:T(1024)S(1)}, f32[640]{0:T(1024)S(1)}, u32[]{:S(2)}, u32[]{:S(2)}) collective-permute-start(f32[640]{0:T(1024)S(1)} %maximum_select_fusion.1), channel_id=1, source_target_pairs={{4,0},{8,4},{12,8},{16,12},{20,16},{24,20},{28,24},{5,1},{9,5},{13... | collective-permute-start | bytes 7688 | tf_op jit(solution)/shard_map/ppermute | solution.py:337
  358.6 3.0 copy-start.2
  360.3 6.4 %collective-permute-start.6 = (f32[512]{0:T(512)S(1)}, f32[512]{0:T(512)S(1)}, u32[]{:S(2)}, u32[]{:S(2)}) collective-permute-start(f32[512]{0:T(512)S(1)} %slice.104), channel_id=1, source_target_pairs={{4,0},{8,4},{12,8},{16,12},{20,16},{24,20},{28,24},{5,1},{9,5},{13... | collective-permute-start | bytes 6152 | tf_op jit(solution)/shard_map/ppermute | solution.py:337
  (32 other events, 33.9 us)
Sparse Core Ops, SparseCore 0:
  9.6 19.4 all-gather.29
  30.6 16.7 all-gather.25
  48.9 16.7 all-gather.27
  98.3 18.5 all-gather.15
  118.4 16.7 all-gather.13
  165.5 28.0 all-gather.19
  195.1 16.7 all-gather.17
  243.7 15.1 all-gather.23
  260.4 16.7 all-gather.21

commit v4 on v3

--- a/solution.py
+++ b/solution.py
@@ -124,10 +124,11 @@
 
 
 def updates_kernel(
-    rows, inverse_ref, left_ref, right_ref, both_ref, vector_ref, logs_ref, tail_ref,
-    up_ref, down_ref, link_ref,
+    rows, inverse_ref, left_ref, right_ref, left_rows_ref, right_rows_ref, vector_ref,
+    logs_ref, tail_ref, up_ref, down_ref, link_ref,
 ):
-    solved = dot(both_ref[...], inverse_ref[...], (1, 0))
+    both = jnp.concatenate([left_rows_ref[...], right_rows_ref[...]])
+    solved = dot(both, inverse_ref[...], (1, 0))
     from_right = dot(solved, right_ref[...], (1, 0))
     up_ref[0:rows, :] = dot(solved[0:rows], left_ref[...], (1, 1))
     link_ref[...] = -from_right[0:rows]
@@ -147,11 +148,11 @@
     return pl.pallas_call(
         functools.partial(updates_kernel, rows),
         out_shape=(message, message, jax.ShapeDtypeStruct((rows, size), jnp.float32)),
-        in_specs=[pl.BlockSpec(memory_space=pltpu.VMEM)] * 7,
+        in_specs=[pl.BlockSpec(memory_space=pltpu.VMEM)] * 8,
         out_specs=(pl.BlockSpec(memory_space=pltpu.VMEM),) * 3,
         compiler_params=pltpu.CompilerParams(vmem_limit_bytes=24 << 20),
     )(
-        inverse, left, right, jnp.concatenate([left_rows, right_rows]),
+        inverse, left, right, left_rows, right_rows,
         jnp.broadcast_to(vector[None], (8, size)), logs, tail,
     )
 
@@ -365,9 +366,12 @@
         )
         return up, down, link, (inverse, left, right, vector)
 
+    pivot, left, right, vector = lax.optimization_barrier((
+        gathered(diag_blocks[1]), coupling[0], coupling[1] * not_last, as_row(rhs[1])
+    ))
+    vector = gathered(vector).reshape(-1, 8, size)[:, 0, :rows].reshape(size)
     up, down, link, chain = eliminated(
-        gathered(diag_blocks[1]), gathered(rhs[1]), coupling[0], coupling[1] * not_last,
-        jnp.zeros((8, size), jnp.float32),
+        pivot, vector, left, right, jnp.zeros((8, size), jnp.float32)
     )
     own = jnp.concatenate([diag_blocks[0], as_row(rhs[0])])
     own, diag, vector, left, right = exchanged(0, 1, True, own, up, down, link)

time: 379 us -> 360 us (0.950)
  local copies, waits for them, and re-layouts: 48.8 us -> 32.8 us
  other arithmetic: 10.1 us -> 2.65 us
  waiting for transfers between devices: 64.8 us -> 71.7 us
  matrix products: 14.1 us -> 9.92 us
    unnamed x80 -> x69, local copies, waits for them, and re-layouts: 29.4 us -> 13.7 us
    concatenate x4 -> x0, other arithmetic: 6.22 us -> none  [updates(): jnp.concatenate([left_rows, right_rows])]
    dot_general x13, matrix products: 14.1 us -> 9.92 us  [product(): return jnp.dot(left_part, right_part, precision=HIGHEST)]
    all_gather x9, waiting for transfers between devices: 49.8 us -> 53.7 us  [gathered(): return lax.all_gather(part, 'rows', axis=0, tiled=True)]
    all_gather x3 -> x4, local copies, waits for them, and re-layouts: 7.74 us -> 8.65 us  [gathered(): return lax.all_gather(part, 'rows', axis=0, tiled=True)]
  transfers between devices with their start and end apart: 16 -> 16, of which waited for: 10 -> 10; matrix products, arithmetic and copies ran while one was open for 7% -> 5% of each run, Pallas kernels for 25% -> 26%
where the time goes in v4:
time: 360 us; the launch traced here: 359 us
  Pallas kernels  210 us (58%)
  waiting for transfers between devices  71.7 us (20%)
  local copies, waits for them, and re-layouts  32.8 us (9%)
  between operations  16.3 us (5%)
  starting transfers between devices  10.5 us (3%)
  matrix products  9.92 us (3%)
  blocking collectives  5.25 us (1%)
    pallas_call x5, Pallas kernels, inverted(): pl.pallas_call(functools.partial(inverse_kernel, size), out_shape=(jax.Sh...  118 us
    pallas_call x4, Pallas kernels, exchanged(): pl.pallas_call(functools.partial(exchange_kernel, stride, local_up, count...  75.6 us
    all_gather x9, waiting for transfers between devices, gathered(): return lax.all_gather(part, 'rows', axis=0, tiled=True)  53.7 us
    pallas_call x4, Pallas kernels, updates(): pl.pallas_call(functools.partial(updates_kernel, rows), out_shape=(messag...  16.3 us
    ppermute x7, waiting for transfers between devices, shifted(): return lax.ppermute(block, axis, route)  15.6 us
    unnamed x69, local copies, waits for them, and re-layouts  13.7 us
    dot_general x13, matrix products, product(): return jnp.dot(left_part, right_part, precision=HIGHEST)  9.92 us
    ppermute x7, starting transfers between devices, shifted(): return lax.ppermute(block, axis, route)  9.69 us
  transfers between devices with their start and end apart: 16, of which 10 were waited for; matrix products, arithmetic and copies ran while one was open for 5% of the time, Pallas kernels for 26%

profile of v4, /device:TPU:0, one launch (start us, length us, event | category | flops | bytes accessed | tf_op | source)
XLA Modules:
  0.0 358.6 jit_solution(6757960704323652092)
XLA Ops:
  11.4 17.6 %all-gather.27.cloned.1.call-done = f32[1,512,512]{2,1,0:T(8,128)} async-done(((f32[1,128,512]{2,1,0:T(8,128)}), f32[1,512,512]{2,1,0:T(8,128)}) %all-gather.27.cloned.1.call-update) | async-done | bytes 1048592 | tf_op jit(solution)/shard_map/all_gather | solution.py:356
  29.9 5.2 %all_gather.33 = f32[32,512]{1,0:T(8,128)S(1)} all-gather(f32[8,512]{1,0:T(8,128)S(1)} %pad.9), channel_id=1, replica_groups=mesh['tm'=8,'rows'=4] {'rows'}, dimensions={0}, use_global_device_ids=true | all-gather | bytes 81920 | tf_op jit(solution)/shard_map/all_gather | solution.py:356
  35.1 23.5 %shard_map.50 = (f32[512,512]{1,0:T(8,128)S(1)}, f32[8,128]{1,0:T(8,128)S(1)}) custom-call(f32[512,512]{1,0:T(8,128)S(1)} %bitcast.88), custom_call_target="tpu_custom_call" | custom-call | flops 10737418240 | bytes 2097152 | tf_op jit(solution)/shard_map/pallas_call | solution.py:106
  61.3 4.5 %all-gather.11.cloned.1.call-done.left_ref = f32[512,512]{1,0:T(8,128)} async-done(((f32[128,512]{1,0:T(8,128)}), f32[512,512]{1,0:T(8,128)}) %all-gather.11.cloned.1.call-update) | async-done | bytes 1048592 | tf_op jit(solution)/shard_map/all_gather | solution.py:356
  67.0 3.3 shard_map.51
  70.4 17.1 %shard_map.52 = (f32[136,512]{1,0:T(8,128)S(1)}, f32[512,512]{1,0:T(8,128)S(1)}, f32[32,512]{1,0:T(8,128)S(1)}, f32[128,512]{1,0:T(8,128)}, f32[128,512]{1,0:T(8,128)S(1)}) custom-call(f32[136,512]{1,0:T(8,128)S(1)} %select_maximum_fusion.own_ref, f32[136,512]{1,0:T(8,128)S(1)} %get-tuple-element.52.up_ref, f32[136,512]{1,0:T(8,128)S(1)} %get-tuple-element.53.down_ref, ...), custom_call_target="tpu_custom_call" | custom-call | tf_op jit(solution)/shard_map/pallas_call | solution.py:302
  90.2 23.5 %shard_map.53 = (f32[512,512]{1,0:T(8,128)S(1)}, f32[8,128]{1,0:T(8,128)S(1)}) custom-call(f32[512,512]{1,0:T(8,128)S(1)} %copy-done.23), custom_call_target="tpu_custom_call" | custom-call | flops 10737418240 | bytes 2097152 | tf_op jit(solution)/shard_map/pallas_call | solution.py:106
  116.3 10.0 %all-gather.15.cloned.1.call-done.left_ref = f32[512,512]{1,0:T(8,128)} async-done(((f32[128,512]{1,0:T(8,128)}), f32[512,512]{1,0:T(8,128)}) %all-gather.15.cloned.1.call-update) | async-done | bytes 1048592 | tf_op jit(solution)/shard_map/all_gather | solution.py:356
  127.6 4.3 %shard_map.54 = (f32[136,512]{1,0:T(8,128)S(1)}, f32[136,512]{1,0:T(8,128)S(1)}, f32[128,512]{1,0:T(8,128)S(1)}) custom-call(f32[512,512]{1,0:T(8,128)S(1)} %get-tuple-element.56.inverse_ref, f32[512,512]{1,0:T(8,128)S(1)} %copy-done.2, f32[512,512]{1,0:T(8,128)S(1)} %copy.8.right_ref, f32[128,512]{1,0:T(8,128)} %get-tuple-element.59.left_rows_ref, ...), custom_call_target="tpu_custom_call" | custom-call | tf_op jit(solution)/shard_map/pallas_call | solution.py:148
  131.9 19.2 %shard_map.55 = (f32[136,512]{1,0:T(8,128)S(1)}, f32[512,512]{1,0:T(8,128)S(1)}, f32[32,512]{1,0:T(8,128)S(1)}, f32[128,512]{1,0:T(8,128)}, f32[128,512]{1,0:T(8,128)S(1)}) custom-call(f32[136,512]{1,0:T(8,128)S(1)} %copy-done.16, f32[136,512]{1,0:T(8,128)S(1)} %get-tuple-element.62.up_ref, f32[136,512]{1,0:T(8,128)S(1)} %get-tuple-element.63.down_ref, ...), custom_call_target="tpu_custom_call" | custom-call | tf_op jit(solution)/shard_map/pallas_call | solution.py:302
  155.0 23.5 %shard_map.56 = (f32[512,512]{1,0:T(8,128)S(1)}, f32[8,128]{1,0:T(8,128)S(1)}) custom-call(f32[512,512]{1,0:T(8,128)S(1)} %copy-done.25), custom_call_target="tpu_custom_call" | custom-call | flops 10737418240 | bytes 2097152 | tf_op jit(solution)/shard_map/pallas_call | solution.py:106
  184.7 14.8 %all-gather.19.cloned.1.call-done.left_ref = f32[512,512]{1,0:T(8,128)} async-done(((f32[128,512]{1,0:T(8,128)}), f32[512,512]{1,0:T(8,128)}) %all-gather.19.cloned.1.call-update) | async-done | bytes 1048592 | tf_op jit(solution)/shard_map/all_gather | solution.py:356
  202.0 4.3 %shard_map.57 = (f32[136,512]{1,0:T(8,128)S(1)}, f32[136,512]{1,0:T(8,128)S(1)}, f32[128,512]{1,0:T(8,128)S(1)}) custom-call(f32[512,512]{1,0:T(8,128)S(1)} %get-tuple-element.66.inverse_ref, f32[512,512]{1,0:T(8,128)S(1)} %copy-done.6, f32[512,512]{1,0:T(8,128)S(1)} %copy-done.12, f32[128,512]{1,0:T(8,128)} %get-tuple-element.69.left_rows_ref, ...), custom_call_target="tpu_custom_call" | custom-call | tf_op jit(solution)/shard_map/pallas_call | solution.py:148
  206.3 19.2 %shard_map.58 = (f32[136,512]{1,0:T(8,128)S(1)}, f32[512,512]{1,0:T(8,128)S(1)}, f32[32,512]{1,0:T(8,128)S(1)}, f32[128,512]{1,0:T(8,128)}, f32[128,512]{1,0:T(8,128)S(1)}) custom-call(f32[136,512]{1,0:T(8,128)S(1)} %copy-done.18, f32[136,512]{1,0:T(8,128)S(1)} %get-tuple-element.72.up_ref, f32[136,512]{1,0:T(8,128)S(1)} %get-tuple-element.73.down_ref, ...), custom_call_target="tpu_custom_call" | custom-call | tf_op jit(solution)/shard_map/pallas_call | solution.py:302
  229.3 23.5 %shard_map.59 = (f32[512,512]{1,0:T(8,128)S(1)}, f32[8,128]{1,0:T(8,128)S(1)}) custom-call(f32[512,512]{1,0:T(8,128)S(1)} %copy-done.27), custom_call_target="tpu_custom_call" | custom-call | flops 10737418240 | bytes 2097152 | tf_op jit(solution)/shard_map/pallas_call | solution.py:106
  252.9 2.9 copy.12.right_ref
  256.8 4.1 %all-gather.23.cloned.1.call-done.left_ref = f32[512,512]{1,0:T(8,128)} async-done(((f32[128,512]{1,0:T(8,128)}), f32[512,512]{1,0:T(8,128)}) %all-gather.23.cloned.1.call-update) | async-done | bytes 1048592 | tf_op jit(solution)/shard_map/all_gather | solution.py:356
  263.4 4.3 %shard_map.60 = (f32[136,512]{1,0:T(8,128)S(1)}, f32[136,512]{1,0:T(8,128)S(1)}, f32[128,512]{1,0:T(8,128)S(1)}) custom-call(f32[512,512]{1,0:T(8,128)S(1)} %get-tuple-element.76.inverse_ref, f32[512,512]{1,0:T(8,128)S(1)} %copy-done.10, f32[512,512]{1,0:T(8,128)S(1)} %copy-done.13, f32[128,512]{1,0:T(8,128)} %get-tuple-element.79.left_rows_ref, ...), custom_call_target="tpu_custom_call" | custom-call | tf_op jit(solution)/shard_map/pallas_call | solution.py:148
  267.7 20.2 %shard_map.61 = (f32[136,512]{1,0:T(8,128)S(1)}, f32[512,512]{1,0:T(8,128)S(1)}, f32[32,512]{1,0:T(8,128)S(1)}, f32[128,512]{1,0:T(8,128)}, f32[128,512]{1,0:T(8,128)}) custom-call(f32[136,512]{1,0:T(8,128)S(1)} %copy-done.20, f32[136,512]{1,0:T(8,128)S(1)} %get-tuple-element.82.up_ref, f32[136,512]{1,0:T(8,128)S(1)} %get-tuple-element.83.down_ref, ...), custom_call_target="tpu_custom_call" | custom-call | tf_op jit(solution)/shard_map/pallas_call | solution.py:302
  287.9 23.5 %shard_map.62 = (f32[512,512]{1,0:T(8,128)S(1)}, f32[8,128]{1,0:T(8,128)S(1)}) custom-call(f32[512,512]{1,0:T(8,128)S(1)} %get-tuple-element.85.matrix_ref), custom_call_target="tpu_custom_call" | custom-call | flops 10737418240 | bytes 2097152 | tf_op jit(solution)/shard_map/pallas_call | solution.py:106
  317.1 4.5 %collective-permute-done.1 = f32[640]{0:T(1024)S(1)} collective-permute-done((f32[640]{0:T(1024)S(1)}, f32[640]{0:T(1024)S(1)}, u32[]{:S(2)}, u32[]{:S(2)}) %collective-permute-start.1) | collective-permute-done | bytes 2592 | tf_op jit(solution)/shard_map/ppermute | solution.py:338
  327.6 3.3 collective-permute-done.3
  336.0 4.6 %collective-permute-done.5 = f32[640]{0:T(1024)S(1)} collective-permute-done((f32[640]{0:T(1024)S(1)}, f32[640]{0:T(1024)S(1)}, u32[]{:S(2)}, u32[]{:S(2)}) %collective-permute-start.5) | collective-permute-done | bytes 2592 | tf_op jit(solution)/shard_map/ppermute | solution.py:338
  345.4 3.2 collective-permute-done.6
  (165 shorter events, 57.9 us)
Async XLA Ops:
  7.2 21.9 %all-gather.27.cloned.1.call-start = ((), (), s32[]{:S(2)}) async-start(), calls=%async_computation.8 | async-start | bytes 1310720 | tf_op jit(solution)/shard_map/all_gather | solution.py:356
  9.1 49.6 %all-gather.13.cloned.1.call-start = ((), (), s32[]{:S(2)}) async-start(), calls=%async_computation.1 | async-start | bytes 1310720 | tf_op jit(solution)/shard_map/all_gather | solution.py:356
  29.0 6.1 %copy-start.21 = (f32[1,512,512]{2,1,0:T(8,128)S(1)}, f32[1,512,512]{2,1,0:T(8,128)}, u32[]{:S(2)}) copy-start(f32[1,512,512]{2,1,0:T(8,128)} %all-gather.27.cloned.1.call-done) | copy-start | bytes 3145732
  29.1 36.7 %all-gather.11.cloned.1.call-start = ((), (), s32[]{:S(2)}) async-start(), calls=%async_computation | async-start | bytes 1310720 | tf_op jit(solution)/shard_map/all_gather | solution.py:356
  29.8 84.0 %all-gather.17.cloned.1.call-start = ((), (), s32[]{:S(2)}) async-start(), calls=%async_computation.3 | async-start | bytes 1310720 | tf_op jit(solution)/shard_map/all_gather | solution.py:356
  89.3 37.0 %all-gather.15.cloned.1.call-start = ((), (), s32[]{:S(2)}) async-start(), calls=%async_computation.2 | async-start | bytes 1310720 | tf_op jit(solution)/shard_map/all_gather | solution.py:356
  89.9 91.2 %all-gather.21.cloned.1.call-start = ((), (), s32[]{:S(2)}) async-start(), calls=%async_computation.5 | async-start | bytes 1310720 | tf_op jit(solution)/shard_map/all_gather | solution.py:356
  153.0 46.6 %all-gather.19.cloned.1.call-start = ((), (), s32[]{:S(2)}) async-start(), calls=%async_computation.4 | async-start | bytes 1310720 | tf_op jit(solution)/shard_map/all_gather | solution.py:356
  153.7 99.2 %all-gather.25.cloned.1.call-start = ((), (), s32[]{:S(2)}) async-start(), calls=%async_computation.7 | async-start | bytes 1310720 | tf_op jit(solution)/shard_map/all_gather | solution.py:356
  178.6 21.0 %copy-start.4 = (f32[512,512]{1,0:T(8,128)}, f32[512,512]{1,0:T(8,128)S(1)}, u32[]{:S(2)}) copy-start(f32[512,512]{1,0:T(8,128)S(1)} %get-tuple-element.66.inverse_ref) | copy-start | bytes 3145732
  227.3 33.6 %all-gather.23.cloned.1.call-start = ((), (), s32[]{:S(2)}) async-start(), calls=%async_computation.6 | async-start | bytes 1310720 | tf_op jit(solution)/shard_map/all_gather | solution.py:356
  252.9 8.1 %copy-start.8 = (f32[512,512]{1,0:T(8,128)}, f32[512,512]{1,0:T(8,128)S(1)}, u32[]{:S(2)}) copy-start(f32[512,512]{1,0:T(8,128)S(1)} %get-tuple-element.76.inverse_ref) | copy-start | bytes 3145732
  313.7 2.8 collective-permute-start
  315.1 6.6 %copy-start.31 = (f32[512,512]{0,1:T(8,128)S(1)}, f32[512,512]{0,1:T(8,128)}, u32[]{:S(2)}) copy-start(f32[512,512]{0,1:T(8,128)} %all-gather.25.cloned.1.call-done) | copy-start | bytes 3145732
  315.1 6.5 %collective-permute-start.1 = (f32[640]{0:T(1024)S(1)}, f32[640]{0:T(1024)S(1)}, u32[]{:S(2)}, u32[]{:S(2)}) collective-permute-start(f32[640]{0:T(1024)S(1)} %concatenate.16), channel_id=1, source_target_pairs={{16,0},{20,4},{24,8},{28,12},{17,1},{21,5},{25,9},{29,13},{18,2},{... | collective-permute-start | bytes 7688 | tf_op jit(solution)/shard_map/ppermute | solution.py:338
  316.5 5.7 %copy-start.9 = (f32[512,512]{1,0:T(8,128)S(1)}, f32[512,512]{1,0:T(8,128)}, u32[]{:S(2)}) copy-start(f32[512,512]{1,0:T(8,128)} %copy-done.8) | copy-start | bytes 3145732
  323.9 3.0 collective-permute-start.2
  325.3 5.6 %copy-start.30 = (f32[512,512]{0,1:T(8,128)S(1)}, f32[512,512]{0,1:T(8,128)}, u32[]{:S(2)}) copy-start(f32[512,512]{0,1:T(8,128)} %all-gather.21.cloned.1.call-done) | copy-start | bytes 3145732
  325.3 5.6 %collective-permute-start.3 = (f32[640]{0:T(1024)S(1)}, f32[640]{0:T(1024)S(1)}, u32[]{:S(2)}, u32[]{:S(2)}) collective-permute-start(f32[640]{0:T(1024)S(1)} %maximum_select_fusion), channel_id=1, source_target_pairs={{8,0},{12,4},{16,8},{20,12},{24,16},{28,20},{9,1},{13,5},{17,9},{2... | collective-permute-start | bytes 7688 | tf_op jit(solution)/shard_map/ppermute | solution.py:338
  332.6 2.8 collective-permute-start.4
  333.9 6.6 %copy-start.29 = (f32[512,512]{0,1:T(8,128)S(1)}, f32[512,512]{0,1:T(8,128)}, u32[]{:S(2)}) copy-start(f32[512,512]{0,1:T(8,128)} %all-gather.17.cloned.1.call-done) | copy-start | bytes 3145732
  333.9 6.6 %collective-permute-start.5 = (f32[640]{0:T(1024)S(1)}, f32[640]{0:T(1024)S(1)}, u32[]{:S(2)}, u32[]{:S(2)}) collective-permute-start(f32[640]{0:T(1024)S(1)} %maximum_select_fusion.1), channel_id=1, source_target_pairs={{4,0},{8,4},{12,8},{16,12},{20,16},{24,20},{28,24},{5,1},{9,5},{13... | collective-permute-start | bytes 7688 | tf_op jit(solution)/shard_map/ppermute | solution.py:338
  341.2 7.4 %copy-start.28 = (f32[512,512]{0,1:T(8,128)S(1)}, f32[512,512]{0,1:T(8,128)}, u32[]{:S(2)}) copy-start(f32[512,512]{0,1:T(8,128)} %all-gather.13.cloned.1.call-done) | copy-start | bytes 3145732
  342.2 6.4 %collective-permute-start.6 = (f32[512]{0:T(512)S(1)}, f32[512]{0:T(512)S(1)}, u32[]{:S(2)}, u32[]{:S(2)}) collective-permute-start(f32[512]{0:T(512)S(1)} %slice.108), channel_id=1, source_target_pairs={{4,0},{8,4},{12,8},{16,12},{20,16},{24,20},{28,24},{5,1},{9,5},{13... | collective-permute-start | bytes 6152 | tf_op jit(solution)/shard_map/ppermute | solution.py:338
  (26 other events, 63.2 us)
Sparse Core Ops, SparseCore 0:
  9.6 19.4 all-gather.26
  30.6 16.8 all-gather.12
  49.0 16.7 all-gather.10
  89.5 18.5 all-gather.16
  109.5 16.7 all-gather.14
  153.1 28.0 all-gather.20
  182.7 16.7 all-gather.18
  227.5 15.1 all-gather.24
  244.2 16.7 all-gather.22

commit v5 on v4

--- a/solution.py
+++ b/solution.py
@@ -124,17 +124,19 @@
 
 
 def updates_kernel(
-    rows, inverse_ref, left_ref, right_ref, left_rows_ref, right_rows_ref, vector_ref,
+    rows, inverse_ref, left_ref, right_ref, left_rows_ref, vector_ref,
     logs_ref, tail_ref, up_ref, down_ref, link_ref,
 ):
-    both = jnp.concatenate([left_rows_ref[...], right_rows_ref[...]])
+    size = up_ref.shape[1]
+    mine = lax.axis_index("rows") * rows + lax.broadcasted_iota(jnp.int32, (rows, size), 0)
+    pick = (lax.broadcasted_iota(jnp.int32, (rows, size), 1) == mine).astype(jnp.float32)
+    both = jnp.concatenate([left_rows_ref[...], dot(pick, right_ref[...], (1, 1))])
     solved = dot(both, inverse_ref[...], (1, 0))
     from_right = dot(solved, right_ref[...], (1, 0))
     up_ref[0:rows, :] = dot(solved[0:rows], left_ref[...], (1, 1))
     link_ref[...] = -from_right[0:rows]
     down_ref[0:rows, :] = from_right[rows:]
     vector = dot(vector_ref[...], solved, (1, 1))
-    size = up_ref.shape[1]
     up_ref[rows:, :] = jnp.zeros((8, size), jnp.float32)
     up_ref[rows:, 0:rows] = vector[:, 0:rows]
     up_ref[rows:, size - TILE:] = logs_ref[...] - tail_ref[:, size - TILE:]
@@ -142,17 +144,17 @@
     down_ref[rows:, 0:rows] = vector[:, rows:]
 
 
-def updates(inverse, left, right, left_rows, right_rows, vector, logs, tail):
+def updates(inverse, left, right, left_rows, vector, logs, tail):
     rows, size = left_rows.shape
     message = jax.ShapeDtypeStruct((rows + 8, size), jnp.float32)
     return pl.pallas_call(
         functools.partial(updates_kernel, rows),
         out_shape=(message, message, jax.ShapeDtypeStruct((rows, size), jnp.float32)),
-        in_specs=[pl.BlockSpec(memory_space=pltpu.VMEM)] * 8,
+        in_specs=[pl.BlockSpec(memory_space=pltpu.VMEM)] * 7,
         out_specs=(pl.BlockSpec(memory_space=pltpu.VMEM),) * 3,
         compiler_params=pltpu.CompilerParams(vmem_limit_bytes=24 << 20),
     )(
-        inverse, left, right, left_rows, right_rows,
+        inverse, left, right, left_rows,
         jnp.broadcast_to(vector[None], (8, size)), logs, tail,
     )
 
@@ -349,9 +351,6 @@
     def my_rows(matrix):
         return lax.dynamic_slice_in_dim(matrix, row_start, rows, 0)
 
-    def my_columns_t(matrix):
-        return lax.dynamic_slice_in_dim(matrix, row_start, rows, 1).T
-
     def gathered(part):
         return lax.all_gather(part, "rows", axis=0, tiled=True)
 
@@ -361,9 +360,7 @@
     def eliminated(diag, vector, left_part, right_part, tail):
         left, right = gathered(left_part), gathered(right_part)
         inverse, logs = inverted(diag)
-        up, down, link = updates(
-            inverse, left, right, left_part, my_columns_t(right), vector, logs, tail
-        )
+        up, down, link = updates(inverse, left, right, left_part, vector, logs, tail)
         return up, down, link, (inverse, left, right, vector)
 
     pivot, left, right, vector = lax.optimization_barrier((

time: 360 us -> 368 us (1.022); the launches traced: 359 us -> 362 us
  local copies, waits for them, and re-layouts: 32.8 us -> 18.3 us
  waiting for transfers between devices: 71.7 us -> 84 us
  Pallas kernels: 210 us -> 214 us
    all_gather x9, waiting for transfers between devices: 53.7 us -> 66 us  [gathered(): return lax.all_gather(part, 'rows', axis=0, tiled=True)]
    all_gather x4 -> x0, local copies, waits for them, and re-layouts: 8.65 us -> none  [gathered(): return lax.all_gather(part, 'rows', axis=0, tiled=True)]
    transpose x4 -> x0, local copies, waits for them, and re-layouts: 3.94 us -> none  [my_columns_t(): return lax.dynamic_slice_in_dim(matrix, row_start, rows, 1).T]
    pallas_call x4, Pallas kernels: 16.3 us -> 20.1 us  [updates(): pl.pallas_call(functools.partial(updates_kernel, rows), out_shape=(messag...]
    unnamed x69 -> x60, local copies, waits for them, and re-layouts: 13.7 us -> 15.1 us
  transfers between devices with their start and end apart: 16 -> 16, of which waited for: 10 -> 10; matrix products, arithmetic and copies ran while one was open for 5% -> 1% of each run, Pallas kernels for 26% -> 26%
where the time goes in v5:
time: 368 us; the launch traced here: 362 us
  Pallas kernels  214 us (58%)
  waiting for transfers between devices  84 us (23%)
  local copies, waits for them, and re-layouts  18.3 us (5%)
  between operations  16.5 us (4%)
  matrix products  11.3 us (3%)
  starting transfers between devices  10.6 us (3%)
  blocking collectives  5.25 us (1%)
    pallas_call x5, Pallas kernels, inverted(): pl.pallas_call(functools.partial(inverse_kernel, size), out_shape=(jax.Sh...  118 us
    pallas_call x4, Pallas kernels, exchanged(): pl.pallas_call(functools.partial(exchange_kernel, stride, local_up, count...  75.9 us
    all_gather x9, waiting for transfers between devices, gathered(): return lax.all_gather(part, 'rows', axis=0, tiled=True)  66 us
    pallas_call x4, Pallas kernels, updates(): pl.pallas_call(functools.partial(updates_kernel, rows), out_shape=(messag...  20.1 us
    ppermute x7, waiting for transfers between devices, shifted(): return lax.ppermute(block, axis, route)  15.6 us
    unnamed x60, local copies, waits for them, and re-layouts  15.1 us
    dot_general x13, matrix products, product(): return jnp.dot(left_part, right_part, precision=HIGHEST)  11.3 us
    ppermute x7, starting transfers between devices, shifted(): return lax.ppermute(block, axis, route)  9.29 us
  transfers between devices with their start and end apart: 16, of which 10 were waited for; matrix products, arithmetic and copies ran while one was open for 1% of the time, Pallas kernels for 26%

profile of v5, /device:TPU:0, one launch (start us, length us, event | category | flops | bytes accessed | tf_op | source)
XLA Modules:
  0.0 362.3 jit_solution(11969856601532290090)
XLA Ops:
  10.7 18.4 %all-gather.27.cloned.1.call-done = f32[1,512,512]{2,1,0:T(8,128)} async-done(((f32[1,128,512]{2,1,0:T(8,128)}), f32[1,512,512]{2,1,0:T(8,128)}) %all-gather.27.cloned.1.call-update) | async-done | bytes 1048592 | tf_op jit(solution)/shard_map/all_gather | solution.py:355
  29.9 5.2 %all_gather.33 = f32[32,512]{1,0:T(8,128)S(1)} all-gather(f32[8,512]{1,0:T(8,128)S(1)} %pad.9), channel_id=1, replica_groups=mesh['tm'=8,'rows'=4] {'rows'}, dimensions={0}, use_global_device_ids=true | all-gather | bytes 81920 | tf_op jit(solution)/shard_map/all_gather | solution.py:355
  35.1 23.5 %shard_map.50 = (f32[512,512]{1,0:T(8,128)S(1)}, f32[8,128]{1,0:T(8,128)S(1)}) custom-call(f32[512,512]{1,0:T(8,128)S(1)} %bitcast.80), custom_call_target="tpu_custom_call" | custom-call | flops 10737418240 | bytes 2097152 | tf_op jit(solution)/shard_map/pallas_call | solution.py:106
  58.7 7.0 %all-gather.13.cloned.1.call-done.right_ref = f32[512,512]{1,0:T(8,128)} async-done(((f32[128,512]{1,0:T(8,128)}), f32[512,512]{1,0:T(8,128)}) %all-gather.13.cloned.1.call-update) | async-done | bytes 1048592 | tf_op jit(solution)/shard_map/all_gather | solution.py:355
  68.2 4.3 %shard_map.51 = (f32[136,512]{1,0:T(8,128)S(1)}, f32[136,512]{1,0:T(8,128)S(1)}, f32[128,512]{1,0:T(8,128)S(1)}) custom-call(f32[512,512]{1,0:T(8,128)S(1)} %get-tuple-element.47.inverse_ref, f32[512,512]{1,0:T(8,128)S(1)} %copy-done.2, f32[512,512]{1,0:T(8,128)S(1)} %copy-done, f32[128,512]{1,0:T(8,128)S(1)} %copy-done.22, ...), custom_call_target="tpu_custom_call" | custom-call | tf_op jit(solution)/shard_map/pallas_call | solution.py:150
  72.5 17.1 %shard_map.52 = (f32[136,512]{1,0:T(8,128)S(1)}, f32[512,512]{1,0:T(8,128)S(1)}, f32[32,512]{1,0:T(8,128)S(1)}, f32[128,512]{1,0:T(8,128)}, f32[128,512]{1,0:T(8,128)}) custom-call(f32[136,512]{1,0:T(8,128)S(1)} %select_maximum_fusion.own_ref, f32[136,512]{1,0:T(8,128)S(1)} %get-tuple-element.52.up_ref, f32[136,512]{1,0:T(8,128)S(1)} %get-tuple-element.53.down_ref, ...), custom_call_target="tpu_custom_call" | custom-call | tf_op jit(solution)/shard_map/pallas_call | solution.py:304
  90.8 23.5 %shard_map.53 = (f32[512,512]{1,0:T(8,128)S(1)}, f32[8,128]{1,0:T(8,128)S(1)}) custom-call(f32[512,512]{1,0:T(8,128)S(1)} %get-tuple-element.55.matrix_ref), custom_call_target="tpu_custom_call" | custom-call | flops 10737418240 | bytes 2097152 | tf_op jit(solution)/shard_map/pallas_call | solution.py:106
  114.4 12.1 %all-gather.17.cloned.1.call-done.right_ref = f32[512,512]{1,0:T(8,128)} async-done(((f32[128,512]{1,0:T(8,128)}), f32[512,512]{1,0:T(8,128)}) %all-gather.17.cloned.1.call-update) | async-done | bytes 1048592 | tf_op jit(solution)/shard_map/all_gather | solution.py:355
  128.9 5.3 %shard_map.54 = (f32[136,512]{1,0:T(8,128)S(1)}, f32[136,512]{1,0:T(8,128)S(1)}, f32[128,512]{1,0:T(8,128)S(1)}) custom-call(f32[512,512]{1,0:T(8,128)S(1)} %get-tuple-element.56.inverse_ref, f32[512,512]{1,0:T(8,128)S(1)} %copy-done.4, f32[512,512]{1,0:T(8,128)S(1)} %copy-done.6, f32[128,512]{1,0:T(8,128)} %get-tuple-element.59.left_rows_ref, ...), custom_call_target="tpu_custom_call" | custom-call | tf_op jit(solution)/shard_map/pallas_call | solution.py:150
  134.2 19.3 %shard_map.55 = (f32[136,512]{1,0:T(8,128)S(1)}, f32[512,512]{1,0:T(8,128)S(1)}, f32[32,512]{1,0:T(8,128)S(1)}, f32[128,512]{1,0:T(8,128)}, f32[128,512]{1,0:T(8,128)}) custom-call(f32[136,512]{1,0:T(8,128)S(1)} %get-tuple-element.58.own_ref, f32[136,512]{1,0:T(8,128)S(1)} %get-tuple-element.62.up_ref, f32[136,512]{1,0:T(8,128)S(1)} %get-tuple-element.63.down_ref, ...), custom_call_target="tpu_custom_call" | custom-call | tf_op jit(solution)/shard_map/pallas_call | solution.py:304
  156.7 23.5 %shard_map.56 = (f32[512,512]{1,0:T(8,128)S(1)}, f32[8,128]{1,0:T(8,128)S(1)}) custom-call(f32[512,512]{1,0:T(8,128)S(1)} %copy-done.25), custom_call_target="tpu_custom_call" | custom-call | flops 10737418240 | bytes 2097152 | tf_op jit(solution)/shard_map/pallas_call | solution.py:106
  180.3 2.3 all-gather.19.cloned.1.call-done.left_ref
  182.6 18.3 %all-gather.21.cloned.1.call-done.right_ref = f32[512,512]{1,0:T(8,128)} async-done(((f32[128,512]{1,0:T(8,128)}), f32[512,512]{1,0:T(8,128)}) %all-gather.21.cloned.1.call-update) | async-done | bytes 1048592 | tf_op jit(solution)/shard_map/all_gather | solution.py:355
  203.4 5.3 %shard_map.57 = (f32[136,512]{1,0:T(8,128)S(1)}, f32[136,512]{1,0:T(8,128)S(1)}, f32[128,512]{1,0:T(8,128)S(1)}) custom-call(f32[512,512]{1,0:T(8,128)S(1)} %get-tuple-element.66.inverse_ref, f32[512,512]{1,0:T(8,128)S(1)} %copy-done.10, f32[512,512]{1,0:T(8,128)S(1)} %copy-done.12, f32[128,512]{1,0:T(8,128)} %get-tuple-element.69.left_rows_ref, ...), custom_call_target="tpu_custom_call" | custom-call | tf_op jit(solution)/shard_map/pallas_call | solution.py:150
  208.6 19.3 %shard_map.58 = (f32[136,512]{1,0:T(8,128)S(1)}, f32[512,512]{1,0:T(8,128)S(1)}, f32[32,512]{1,0:T(8,128)S(1)}, f32[128,512]{1,0:T(8,128)}, f32[128,512]{1,0:T(8,128)}) custom-call(f32[136,512]{1,0:T(8,128)S(1)} %get-tuple-element.68.own_ref, f32[136,512]{1,0:T(8,128)S(1)} %get-tuple-element.72.up_ref, f32[136,512]{1,0:T(8,128)S(1)} %get-tuple-element.73.down_ref, ...), custom_call_target="tpu_custom_call" | custom-call | tf_op jit(solution)/shard_map/pallas_call | solution.py:304
  230.9 23.5 %shard_map.59 = (f32[512,512]{1,0:T(8,128)S(1)}, f32[8,128]{1,0:T(8,128)S(1)}) custom-call(f32[512,512]{1,0:T(8,128)S(1)} %copy-done.27), custom_call_target="tpu_custom_call" | custom-call | flops 10737418240 | bytes 2097152 | tf_op jit(solution)/shard_map/pallas_call | solution.py:106
  254.5 7.9 %all-gather.25.cloned.1.call-done.right_ref = f32[512,512]{1,0:T(8,128)} async-done(((f32[128,512]{1,0:T(8,128)}), f32[512,512]{1,0:T(8,128)}) %all-gather.25.cloned.1.call-update) | async-done | bytes 1048592 | tf_op jit(solution)/shard_map/all_gather | solution.py:355
  264.9 5.3 %shard_map.60 = (f32[136,512]{1,0:T(8,128)S(1)}, f32[136,512]{1,0:T(8,128)S(1)}, f32[128,512]{1,0:T(8,128)S(1)}) custom-call(f32[512,512]{1,0:T(8,128)S(1)} %get-tuple-element.76.inverse_ref, f32[512,512]{1,0:T(8,128)S(1)} %copy-done.16, f32[512,512]{1,0:T(8,128)S(1)} %copy-done.18, f32[128,512]{1,0:T(8,128)} %get-tuple-element.79.left_rows_ref, ...), custom_call_target="tpu_custom_call" | custom-call | tf_op jit(solution)/shard_map/pallas_call | solution.py:150
  270.1 20.2 %shard_map.61 = (f32[136,512]{1,0:T(8,128)S(1)}, f32[512,512]{1,0:T(8,128)S(1)}, f32[32,512]{1,0:T(8,128)S(1)}, f32[128,512]{1,0:T(8,128)}, f32[128,512]{1,0:T(8,128)}) custom-call(f32[136,512]{1,0:T(8,128)S(1)} %get-tuple-element.78.own_ref, f32[136,512]{1,0:T(8,128)S(1)} %get-tuple-element.82.up_ref, f32[136,512]{1,0:T(8,128)S(1)} %get-tuple-element.83.down_ref, ...), custom_call_target="tpu_custom_call" | custom-call | tf_op jit(solution)/shard_map/pallas_call | solution.py:304
  290.4 23.5 %shard_map.62 = (f32[512,512]{1,0:T(8,128)S(1)}, f32[8,128]{1,0:T(8,128)S(1)}) custom-call(f32[512,512]{1,0:T(8,128)S(1)} %get-tuple-element.85.matrix_ref), custom_call_target="tpu_custom_call" | custom-call | flops 10737418240 | bytes 2097152 | tf_op jit(solution)/shard_map/pallas_call | solution.py:106
  319.4 4.5 %collective-permute-done.1 = f32[640]{0:T(1024)S(1)} collective-permute-done((f32[640]{0:T(1024)S(1)}, f32[640]{0:T(1024)S(1)}, u32[]{:S(2)}, u32[]{:S(2)}) %collective-permute-start.1) | collective-permute-done | bytes 2592 | tf_op jit(solution)/shard_map/ppermute | solution.py:340
  330.1 3.3 collective-permute-done.3
  338.7 4.6 %collective-permute-done.5 = f32[640]{0:T(1024)S(1)} collective-permute-done((f32[640]{0:T(1024)S(1)}, f32[640]{0:T(1024)S(1)}, u32[]{:S(2)}, u32[]{:S(2)}) %collective-permute-start.5) | collective-permute-done | bytes 2592 | tf_op jit(solution)/shard_map/ppermute | solution.py:340
  348.5 3.2 collective-permute-done.6
  (144 shorter events, 45.4 us)
Async XLA Ops:
  7.2 21.9 %all-gather.27.cloned.1.call-start = ((), (), s32[]{:S(2)}) async-start(), calls=%async_computation.8 | async-start | bytes 1310720 | tf_op jit(solution)/shard_map/all_gather | solution.py:355
  9.1 49.6 %all-gather.11.cloned.1.call-start = ((), (), s32[]{:S(2)}) async-start(), calls=%async_computation | async-start | bytes 1310720 | tf_op jit(solution)/shard_map/all_gather | solution.py:355
  29.1 36.6 %all-gather.13.cloned.1.call-start = ((), (), s32[]{:S(2)}) async-start(), calls=%async_computation.1 | async-start | bytes 1310720 | tf_op jit(solution)/shard_map/all_gather | solution.py:355
  29.8 84.6 %all-gather.15.cloned.1.call-start = ((), (), s32[]{:S(2)}) async-start(), calls=%async_computation.2 | async-start | bytes 1310720 | tf_op jit(solution)/shard_map/all_gather | solution.py:355
  35.1 30.6 %copy-start.22 = (f32[128,512]{1,0:T(8,128)S(1)}, f32[128,512]{1,0:T(8,128)}, u32[]{:S(2)}) copy-start(f32[128,512]{1,0:T(8,128)} %get-tuple-element.48.left_rows_ref) | copy-start | bytes 786436
  89.6 36.8 %all-gather.17.cloned.1.call-start = ((), (), s32[]{:S(2)}) async-start(), calls=%async_computation.3 | async-start | bytes 1310720 | tf_op jit(solution)/shard_map/all_gather | solution.py:355
  90.2 92.3 %all-gather.19.cloned.1.call-start = ((), (), s32[]{:S(2)}) async-start(), calls=%async_computation.4 | async-start | bytes 1310720 | tf_op jit(solution)/shard_map/all_gather | solution.py:355
  114.4 19.8 %copy-start.8 = (f32[512,512]{1,0:T(8,128)}, f32[512,512]{1,0:T(8,128)S(1)}, u32[]{:S(2)}) copy-start(f32[512,512]{1,0:T(8,128)S(1)} %get-tuple-element.56.inverse_ref) | copy-start | bytes 3145732
  154.5 46.4 %all-gather.21.cloned.1.call-start = ((), (), s32[]{:S(2)}) async-start(), calls=%async_computation.5 | async-start | bytes 1310720 | tf_op jit(solution)/shard_map/all_gather | solution.py:355
  155.3 99.2 %all-gather.23.cloned.1.call-start = ((), (), s32[]{:S(2)}) async-start(), calls=%async_computation.6 | async-start | bytes 1310720 | tf_op jit(solution)/shard_map/all_gather | solution.py:355
  180.3 28.3 %copy-start.14 = (f32[512,512]{1,0:T(8,128)}, f32[512,512]{1,0:T(8,128)S(1)}, u32[]{:S(2)}) copy-start(f32[512,512]{1,0:T(8,128)S(1)} %get-tuple-element.66.inverse_ref) | copy-start | bytes 3145732
  228.9 33.5 %all-gather.25.cloned.1.call-start = ((), (), s32[]{:S(2)}) async-start(), calls=%async_computation.7 | async-start | bytes 1310720 | tf_op jit(solution)/shard_map/all_gather | solution.py:355
  254.5 15.7 %copy-start.20 = (f32[512,512]{1,0:T(8,128)}, f32[512,512]{1,0:T(8,128)S(1)}, u32[]{:S(2)}) copy-start(f32[512,512]{1,0:T(8,128)S(1)} %get-tuple-element.76.inverse_ref) | copy-start | bytes 3145732
  314.5 9.4 %copy-start.19 = (f32[512,512]{1,0:T(8,128)S(1)}, f32[512,512]{1,0:T(8,128)}, u32[]{:S(2)}) copy-start(f32[512,512]{1,0:T(8,128)} %all-gather.25.cloned.1.call-done.right_ref) | copy-start | bytes 3145732
  316.2 2.6 collective-permute-start
  317.5 6.4 %collective-permute-start.1 = (f32[640]{0:T(1024)S(1)}, f32[640]{0:T(1024)S(1)}, u32[]{:S(2)}, u32[]{:S(2)}) collective-permute-start(f32[640]{0:T(1024)S(1)} %concatenate.16), channel_id=1, source_target_pairs={{16,0},{20,4},{24,8},{28,12},{17,1},{21,5},{25,9},{29,13},{18,2},{... | collective-permute-start | bytes 7688 | tf_op jit(solution)/shard_map/ppermute | solution.py:340
  324.9 8.5 %copy-start.13 = (f32[512,512]{1,0:T(8,128)S(1)}, f32[512,512]{1,0:T(8,128)}, u32[]{:S(2)}) copy-start(f32[512,512]{1,0:T(8,128)} %all-gather.21.cloned.1.call-done.right_ref) | copy-start | bytes 3145732
  326.6 2.9 collective-permute-start.2
  327.9 5.5 %collective-permute-start.3 = (f32[640]{0:T(1024)S(1)}, f32[640]{0:T(1024)S(1)}, u32[]{:S(2)}, u32[]{:S(2)}) collective-permute-start(f32[640]{0:T(1024)S(1)} %maximum_select_fusion), channel_id=1, source_target_pairs={{8,0},{12,4},{16,8},{20,12},{24,16},{28,20},{9,1},{13,5},{17,9},{2... | collective-permute-start | bytes 7688 | tf_op jit(solution)/shard_map/ppermute | solution.py:340
  334.4 8.8 %copy-start.7 = (f32[512,512]{1,0:T(8,128)S(1)}, f32[512,512]{1,0:T(8,128)}, u32[]{:S(2)}) copy-start(f32[512,512]{1,0:T(8,128)} %all-gather.17.cloned.1.call-done.right_ref) | copy-start | bytes 3145732
  335.4 2.6 collective-permute-start.4
  336.7 6.5 %collective-permute-start.5 = (f32[640]{0:T(1024)S(1)}, f32[640]{0:T(1024)S(1)}, u32[]{:S(2)}, u32[]{:S(2)}) collective-permute-start(f32[640]{0:T(1024)S(1)} %maximum_select_fusion.1), channel_id=1, source_target_pairs={{4,0},{8,4},{12,8},{16,12},{20,16},{24,20},{28,24},{5,1},{9,5},{13... | collective-permute-start | bytes 7688 | tf_op jit(solution)/shard_map/ppermute | solution.py:340
  344.3 7.4 %copy-start.1 = (f32[512,512]{1,0:T(8,128)S(1)}, f32[512,512]{1,0:T(8,128)}, u32[]{:S(2)}) copy-start(f32[512,512]{1,0:T(8,128)} %all-gather.13.cloned.1.call-done.right_ref) | copy-start | bytes 3145732
  345.3 6.4 %collective-permute-start.6 = (f32[512]{0:T(512)S(1)}, f32[512]{0:T(512)S(1)}, u32[]{:S(2)}, u32[]{:S(2)}) collective-permute-start(f32[512]{0:T(512)S(1)} %slice.108), channel_id=1, source_target_pairs={{4,0},{8,4},{12,8},{16,12},{20,16},{24,20},{28,24},{5,1},{9,5},{13... | collective-permute-start | bytes 6152 | tf_op jit(solution)/shard_map/ppermute | solution.py:340
  (22 other events, 59.4 us)
Sparse Core Ops, SparseCore 0:
  9.6 19.4 all-gather.26
  30.6 16.7 all-gather.10
  48.9 16.7 all-gather.12
  89.8 18.4 all-gather.14
  109.6 16.7 all-gather.16
  154.6 27.8 all-gather.18
  184.1 16.7 all-gather.20
  229.1 15.0 all-gather.22
  245.7 16.6 all-gather.24
